TPU v7x, 256 devices: a whole 4x4x8 slice. The times are simulated.
256 devices in a mesh: section: 64 (over x, z, y_hi), tp: 4 (over y_lo, core).
Axes of the slice: x: 4, y: 4 (y_hi: 2, y_lo: 2; y = y_hi * 2 + y_lo), z: 8, core: 2. Of those that a mesh axis runs over, the one named last changes fastest.
Arguments:
- query: bfloat16 [64, 2, 256, 4096], P('section', None, None, 'tp'), may hold values from -6 to 6
- keyval: bfloat16 [64, 768, 1024], P('section', None, 'tp'), may hold values from -6 to 6
- q_weight: bfloat16 [64, 4096, 4096], P('section', None, 'tp'), may hold values from -0.09375 to 0.09375
- kv_weight: bfloat16 [64, 4096, 1024], P('section', None, 'tp'), may hold values from -0.09375 to 0.09375
- block_index: int32 [64], P('section'), may hold values from 0 to 1
- carry_in: bfloat16 [64, 768, 1024], P('section', None, 'tp'), may hold values from -0.59765625 to 0.59765625
- grad_late: bfloat16 [64, 256, 4096], P('section', None, 'tp'), may hold values from -6 to 6
- grad_top: bfloat16 [256, 4096], P(None, 'tp'), may hold values from -6 to 6
Outputs:
- grad_early: bfloat16 [64, 256, 4096], P('section', None, 'tp')
- carry_out: bfloat16 [64, 768, 1024], P('section', None, 'tp')
All inputs are finite; a program needn't handle non-finite values.
Results may differ from a plain program's by a relative error of at most 0.02.
Values may be sent and summed in bfloat16 or wider, within the bound.
No kernel may reach another device: no remote copies, remote signals or barrier semaphores. Data moves between devices by JAX's collectives and lax.ppermute only.
A program may use at most 64 MiB of HBM per device.

v0:
```python
import math

import jax
import jax.numpy as jnp
from jax import lax
from jax.sharding import PartitionSpec as P

HD = 128


def passed_along(block, axis, distance):
    devices = range(lax.axis_size(axis))
    route = [(i - distance, i) for i in devices if i - distance in devices]
    return lax.ppermute(block, axis, route)


def block_terms(queries, gradient, keyval, first_row):
    row_count = queries.shape[0]
    length = keyval.shape[0]
    kv_local = keyval.shape[1] // (2 * HD)
    group_size = queries.shape[1] // (kv_local * HD)
    score_scale = 1.0 / math.sqrt(HD)
    q_heads = queries.reshape(row_count, kv_local, group_size, HD)
    grad_heads = gradient.reshape(row_count, kv_local, group_size, HD)
    kv_pairs = keyval.reshape(length, kv_local, 2, HD)
    key_rows = kv_pairs[:, :, 0]
    value_rows = kv_pairs[:, :, 1]
    scores = (
        jnp.einsum("rgjd,tgd->grjt", q_heads, key_rows, preferred_element_type=jnp.float32)
        * score_scale
    )
    positions = first_row + jnp.arange(row_count, dtype=jnp.int32)
    visible = (jnp.arange(length, dtype=jnp.int32)[None, :] <= positions[:, None])[None, :, None, :]
    masked = jnp.where(visible, scores, -1e30)
    highest = jnp.max(masked, axis=-1, keepdims=True)
    exponent = jnp.exp(masked - highest)
    attn_probs = exponent / jnp.sum(exponent, axis=-1, keepdims=True)
    probs_low = attn_probs.astype(jnp.bfloat16)
    value_terms = jnp.einsum(
        "grjt,rgjd->tgd", probs_low, grad_heads, preferred_element_type=jnp.float32
    )
    grad_probs = jnp.einsum(
        "rgjd,tgd->grjt", grad_heads, value_rows, preferred_element_type=jnp.float32
    )
    row_delta = jnp.sum(attn_probs * grad_probs, axis=-1, keepdims=True)
    grad_scores = (attn_probs * (grad_probs - row_delta)).astype(jnp.bfloat16)
    grad_query = (
        jnp.einsum("grjt,tgd->rgjd", grad_scores, key_rows, preferred_element_type=jnp.float32)
        * score_scale
    )
    key_terms = (
        jnp.einsum("grjt,rgjd->tgd", grad_scores, q_heads, preferred_element_type=jnp.float32)
        * score_scale
    )
    kv_terms = jnp.stack([key_terms, value_terms], axis=2).reshape(length, -1)
    return (grad_query.astype(jnp.bfloat16).reshape(row_count, -1), kv_terms)


def project(grad_query, own_rows, q_local, kv_local):
    contract_dims = (((1,), (1,)), ((), ()))
    summed = lax.dot_general(grad_query, q_local, contract_dims, preferred_element_type=jnp.float32)
    return summed + lax.dot_general(
        own_rows, kv_local, contract_dims, preferred_element_type=jnp.float32
    )


def tensor_total(partial_sum):
    full_sum = lax.psum(partial_sum.astype(jnp.bfloat16), "tp").astype(jnp.float32)
    shard_width = partial_sum.shape[1] // lax.axis_size("tp")
    return lax.dynamic_slice_in_dim(full_sum, lax.axis_index("tp") * shard_width, shard_width, 1)


def local(query, keyval, q_weight, kv_weight, block_index, carry_in, grad_late, grad_top):
    row_count = grad_late.shape[1]
    length = keyval.shape[1]
    block_at = block_index[0]
    late_first = (block_at + 1) * row_count
    early_first = block_at * row_count
    kv_pairs = keyval[0]
    q_local = q_weight[0]
    kv_local = kv_weight[0]
    late_query, late_terms = block_terms(query[0, 0], grad_late[0], kv_pairs, late_first)
    running = carry_in[0].astype(jnp.float32) + late_terms
    late_own = lax.dynamic_slice_in_dim(running, late_first, row_count, 0).astype(jnp.bfloat16)
    late_sum = tensor_total(project(late_query, late_own, q_local, kv_local))
    late_dx = (grad_late[0].astype(jnp.float32) + late_sum).astype(jnp.bfloat16)
    received = passed_along(late_dx, "section", -1)
    is_last = lax.axis_index("section") == lax.axis_size("section") - 1
    early_grad = jnp.where(is_last, grad_top, received)
    early_query, early_terms = block_terms(query[0, 1], early_grad, kv_pairs, early_first)
    running = running + early_terms
    early_own = lax.dynamic_slice_in_dim(running, early_first, row_count, 0).astype(jnp.bfloat16)
    early_sum = tensor_total(project(early_query, early_own, q_local, kv_local))
    early_dx = (early_grad.astype(jnp.float32) + early_sum).astype(jnp.bfloat16)
    below = jnp.arange(length, dtype=jnp.int32)[:, None] < early_first
    carried_out = jnp.where(below, running, jnp.zeros_like(running)).astype(jnp.bfloat16)
    return (early_dx[None], carried_out[None])


def solution(mesh):
    in_specs = (
        P("section", None, None, "tp"),
        P("section", None, "tp"),
        P("section", None, "tp"),
        P("section", None, "tp"),
        P("section"),
        P("section", None, "tp"),
        P("section", None, "tp"),
        P(None, "tp"),
    )
    out_specs = (P("section", None, "tp"), P("section", None, "tp"))
    return jax.shard_map(local, mesh=mesh, in_specs=in_specs, out_specs=out_specs, check_vma=False)
```

profile of v0, /device:TPU:1, one launch (start us, length us, event | category | flops | bytes accessed | tf_op | source)
XLA Modules:
  0.0 228.3 jit_solution(753918958618960881)
XLA Ops:
  7.2 0.0 copy-start
  7.2 0.0 all-reduce.3.cloned.1.call-start
  7.2 2.1 copy.23
  9.9 0.2 iota_compare_fusion.1
  10.1 2.1 fusion.59
  12.2 0.2 copy.47
  12.4 1.2 copy.51
  13.6 6.0 %fusion.60 = (f32[256,8]{0,1:T(8,128)S(1)}, f32[256,8,768]{2,0,1:T(8,128)}) fusion(pred[256,768]{1,0:T(8,128)(4,1)S(1)} %iota_compare_fusion.1, bf16[256,8,128]{0,2,1:T(8,128)(2,1)S(1)} %bitcast.168, bf16[768,1,2,128]{0,3,2,1:T(8,128)(2,1)} %bitcast.173), kind=kOutput, calls=%fused_computation.86 | convolution fusion | flops 408945408 | bytes 7217152 | tf_op jit(solution)/shard_map/sub | solution.py:36
  19.7 3.8 %multiply_reduce_fusion.1 = (f32[256,8]{0,1:T(8,128)S(1)}, f32[256,8,768]{2,0,1:T(8,128)S(1)}) fusion(f32[256,8,768]{2,0,1:T(8,128)} %get-tuple-element.7, f32[256,8]{0,1:T(8,128)S(1)} %get-tuple-element.6, bf16[256,8,128]{0,2,1:T(8,128)(2,1)S(1)} %bitcast.170, bf16[768,1,2,128]{0,3,2,1:T(8,128)(2,1)} %bitcast.174), kind=kOutput, calls=%fused_computation.11 | convolution fusion | flops 407369728 | bytes 13320192 | tf_op jit(solution)/shard_map/rgjd,tgd->grjt/dot_general | solution.py:42
  23.5 0.9 copy-done.1
  24.4 0.9 fusion.24
  25.3 1.2 multiply_convert_fusion.1
  26.5 0.6 fusion.31
  27.1 2.0 fusion.22
  29.1 0.1 pad_maximum_fusion
  29.1 1.1 copy.30
  30.3 2.1 fusion.35
  32.4 7.9 %fusion.4 = f32[256,4096]{1,0:T(8,128)} fusion(bf16[256,1024]{0,1:T(8,128)(2,1)} %bitcast.180, bf16[1,4096,1024]{2,1,0:T(8,128)(2,1)} %param.10), kind=kOutput, calls=%fused_computation.4 | convolution fusion | flops 2147483648 | bytes 13107200 | tf_op jit(solution)/shard_map/dot_general | solution.py:61
  40.3 4.4 %fusion.6 = bf16[256,4096]{1,0:T(8,128)(2,1)} fusion(f32[256,4096]{1,0:T(8,128)} %fusion.4, bf16[1,4096,256]{2,1,0:T(8,128)(2,1)S(1)} %copy-done, f32[768,256]{1,0:T(8,128)} %fusion.35, s32[]{:T(128)S(6)} %select_n.34), kind=kOutput, calls=%fused_computation.16 | convolution fusion | flops 538968064 | bytes 8519684 | tf_op jit(solution)/shard_map/dot_general | solution.py:62
  44.6 0.0 all-reduce.3.cloned.1.call-update
  44.7 0.0 all-reduce.5.cloned.1.call-start
  44.7 2.0 copy.50
  46.8 64.7 %all-reduce.3.cloned.1.call-done = bf16[256,4096]{1,0:T(8,128)(2,1)} async-done(((bf16[256,4096]{1,0:T(8,128)(2,1)}), bf16[256,4096]{1,0:T(8,128)(2,1)}) %all-reduce.3.cloned.1.call-update) | async-done | bytes 2097168 | tf_op jit(solution)/shard_map/psum | solution.py:68
  111.5 2.0 fusion.34
  113.5 1.5 collective-permute-start
  115.0 0.2 iota_compare_fusion
  115.2 6.2 %fusion.61 = (f32[256,8]{0,1:T(8,128)S(1)}, f32[256,8,768]{2,0,1:T(8,128)}) fusion(pred[256,768]{1,0:T(8,128)(4,1)S(1)} %iota_compare_fusion, bf16[256,8,128]{0,2,1:T(8,128)(2,1)} %bitcast.166, bf16[768,1,2,128]{0,3,2,1:T(8,128)(2,1)} %bitcast.175), kind=kOutput, calls=%fused_computation.87 | convolution fusion | flops 408945408 | bytes 7217152 | tf_op jit(solution)/shard_map/sub | solution.py:36
  121.4 9.0 %collective-permute-done = bf16[256,1024]{1,0:T(8,128)(2,1)} collective-permute-done((bf16[256,1024]{1,0:T(8,128)(2,1)}, bf16[256,1024]{1,0:T(8,128)(2,1)}, u32[]{:S(2)}, u32[]{:S(2)}) %collective-permute-start) | collective-permute-done | bytes 524320 | tf_op jit(solution)/shard_map/ppermute | solution.py:14
  130.4 1.2 broadcast_select_fusion
  131.7 3.7 %multiply_reduce_fusion = (f32[256,8]{0,1:T(8,128)S(1)}, f32[256,8,768]{2,0,1:T(8,128)S(1)}) fusion(f32[256,8,768]{2,0,1:T(8,128)} %get-tuple-element.11, f32[256,8]{0,1:T(8,128)S(1)} %get-tuple-element.10, bf16[768,1,2,128]{0,3,2,1:T(8,128)(2,1)} %bitcast.176, bf16[256,1024]{1,0:T(8,128)(2,1)S(1)} %broadcast_select_fusion), kind=kOutput, calls=%fused_computation.7 | convolution fusion | flops 407369728 | bytes 13320192 | tf_op jit(solution)/shard_map/rgjd,tgd->grjt/dot_general | solution.py:42
  135.4 0.1 slice-done.1
  135.6 1.2 fusion.58
  136.8 0.6 fusion.33
  137.4 1.9 fusion.23
  139.4 0.1 copy.54
  139.5 2.0 fusion.27
  141.5 0.1 pad_maximum_fusion.1
  141.6 0.9 copy-done.2
  142.5 0.7 constant_dynamic-slice_fusion
  143.2 1.8 copy.52
  145.0 6.0 %fusion.2 = f32[256,4096]{1,0:T(8,128)S(1)} fusion(bf16[256,1024]{0,1:T(8,128)(2,1)} %bitcast.179, bf16[1,4096,1024]{2,1,0:T(8,128)(2,1)} %param.10), kind=kOutput, calls=%fused_computation.2 | convolution fusion | flops 2147483648 | bytes 13107200 | tf_op jit(solution)/shard_map/dot_general | solution.py:61
  151.0 3.0 %fusion.7 = bf16[256,4096]{1,0:T(8,128)(2,1)} fusion(f32[256,4096]{1,0:T(8,128)S(1)} %fusion.2, bf16[1,4096,256]{2,1,0:T(8,128)(2,1)S(1)} %copy-done, f32[256,256]{1,0:T(8,128)S(1)} %copy-done.6, f32[768,256]{1,0:T(8,128)} %fusion.35, s32[]{:T(128)S(6)} %select_n.38), kind=kOutput, calls=%fused_computation.17 | convolution fusion | flops 539099136 | bytes 8912900 | tf_op jit(solution)/shard_map/dot_general | solution.py:62
  154.0 0.0 all-reduce.5.cloned.1.call-update
  154.0 1.2 copy.37
  155.2 1.4 copy.38
  156.6 2.2 fusion.38
  158.8 60.7 %all-reduce.5.cloned.1.call-done = bf16[256,4096]{1,0:T(8,128)(2,1)} async-done(((bf16[256,4096]{1,0:T(8,128)(2,1)}), bf16[256,4096]{1,0:T(8,128)(2,1)}) %all-reduce.5.cloned.1.call-update) | async-done | bytes 2097168 | tf_op jit(solution)/shard_map/psum | solution.py:68
  219.4 2.0 fusion.43
  (22 shorter events, 0.1 us)
Async XLA Ops:
  7.2 33.1 %copy-start = (bf16[1,4096,256]{2,1,0:T(8,128)(2,1)S(1)}, bf16[1,4096,256]{2,1,0:T(8,128)(2,1)}, u32[]{:S(2)}) copy-start(bf16[1,4096,256]{2,1,0:T(8,128)(2,1)} %param.11) | copy-start | bytes 6291460
  7.2 104.3 %all-reduce.3.cloned.1.call-start = ((), (), s32[]{:S(2)}) async-start(), calls=%async_computation | async-start | bytes 4194304 | tf_op jit(solution)/shard_map/psum | solution.py:68
  19.7 4.7 %copy-start.1 = (f32[256,8,768]{2,0,1:T(8,128)S(1)}, f32[256,8,768]{2,0,1:T(8,128)}, u32[]{:S(2)}) copy-start(f32[256,8,768]{2,0,1:T(8,128)} %get-tuple-element.7) | copy-start | bytes 18874372
  25.3 1.8 copy-start.7
  27.1 3.2 %copy-start.5 = (bf16[1,768,256]{2,1,0:T(8,128)(2,1)S(1)}, bf16[1,768,256]{2,1,0:T(8,128)(2,1)}, u32[]{:S(2)}) copy-start(bf16[1,768,256]{2,1,0:T(8,128)(2,1)} %param.13) | copy-start | bytes 1179652
  40.2 71.2 %copy-start.3 = (bf16[1,256,1024]{2,1,0:T(8,128)(2,1)S(1)}, bf16[1,256,1024]{2,1,0:T(8,128)(2,1)}, u32[]{:S(2)}) copy-start(bf16[1,256,1024]{2,1,0:T(8,128)(2,1)} %param.14) | copy-start | bytes 1572868
  44.7 174.8 %all-reduce.5.cloned.1.call-start = ((), (), s32[]{:S(2)}) async-start(), calls=%async_computation.1 | async-start | bytes 4194304 | tf_op jit(solution)/shard_map/psum | solution.py:68
  113.5 16.9 %collective-permute-start = (bf16[256,1024]{1,0:T(8,128)(2,1)}, bf16[256,1024]{1,0:T(8,128)(2,1)}, u32[]{:S(2)}, u32[]{:S(2)}) collective-permute-start(bf16[256,1024]{1,0:T(8,128)(2,1)} %fusion.34), channel_id=1, source_target_pairs={{4,0},{8,4},{12,8},{16,12},{20,16},{24,20},{28,24},{32,28},{36,32}... | collective-permute-start | bytes 1572872 | tf_op jit(solution)/shard_map/ppermute | solution.py:14
  130.4 5.0 %slice-start = ((s8[6291456]{0:T(1024)(128)(4,1)}), s8[4194304]{0:T(1024)(128)(4,1)S(1)}, s32[]{:S(2)}) async-start(s8[6291456]{0:T(1024)(128)(4,1)} %bitcast.161), calls=%async_computation.2 | async-start | bytes 8388608
  131.7 3.9 %slice-start.1 = ((s8[6291456]{0:T(1024)(128)(4,1)}), s8[2097152]{0:T(1024)(128)(4,1)S(1)}, s32[]{:S(2)}) async-start(s8[6291456]{0:T(1024)(128)(4,1)} %bitcast.161), calls=%async_computation.3 | async-start | bytes 4194304
  135.6 1.3 copy-start.4
  135.6 1.9 copy-start.8
  141.6 0.9 copy-start.2
  145.0 6.0 %copy-start.6 = (f32[256,256]{1,0:T(8,128)S(1)}, f32[256,256]{1,0:T(8,128)}, u32[]{:S(2)}) copy-start(f32[256,256]{1,0:T(8,128)} %copy.52) | copy-start | bytes 786436
Sparse Core Ops, SparseCore 0:
  44.8 66.6 all-reduce.2
  154.2 65.2 all-reduce.4
where the time goes:
time: 229 us; the launch traced here: 228 us
  waiting for transfers between devices  134 us (59%)
  matrix products  49.1 us (21%)
  local copies, waits for them, and re-layouts  15.9 us (7%)
  between operations  14.9 us (7%)
  other arithmetic  12.4 us (5%)
    psum x2, waiting for transfers between devices, tensor_total(): lax.psum(partial_sum.astype(jnp.bfloat16), 'tp').astype(jnp.float32)  125 us
    dot_general x2, matrix products, project(): lax.dot_general(grad_query, q_local, contract_dims, preferred_element_typ...  13.9 us
    sub x2, matrix products, block_terms(): exponent = jnp.exp(masked - highest)  12.2 us
    ppermute x1, waiting for transfers between devices, passed_along(): return lax.ppermute(block, axis, route)  9.04 us
    unnamed x27, local copies, waits for them, and re-layouts  8.14 us
    dot_general x2, matrix products, block_terms(): jnp.einsum('rgjd,tgd->grjt', grad_heads, value_rows, preferred_element_ty...  7.52 us
    dot_general x2, matrix products, project(): lax.dot_general(own_rows, kv_local, contract_dims, preferred_element_type...  7.43 us
  transfers between devices with their start and end apart: 3, of which 3 were waited for; matrix products, arithmetic and copies ran while one was open for 6% of the time, Pallas kernels for 0%

commit v1 on v0

v1 whole, which is shorter than its diff:
```python
import functools
import math

import jax
import jax.numpy as jnp
from jax import lax
from jax.experimental import pallas as pl
from jax.experimental.pallas import tpu as pltpu
from jax.sharding import PartitionSpec as P

HD = 128
BLOCK = 256
WIDTH = 1024
KV_WIDTH = 256
CHUNKS = ((128, 256), (0, 128))
NT = (((1,), (1,)), ((), ()))
NN = (((1,), (0,)), ((), ()))


def dot(a, b, dims=NN):
    return lax.dot_general(a, b, dims, preferred_element_type=jnp.float32)


def attend(q, do, kv_ref, visible_to, keys, dq_ref, pairs, running):
    rows = q.shape[0]
    heads = q.shape[1] // HD
    scale = 1.0 / math.sqrt(HD)
    key_rows = kv_ref[:keys, :HD]
    value_rows = kv_ref[:keys, HD:]
    keys_t = key_rows.astype(jnp.float32).T.astype(jnp.bfloat16)
    lane = lax.broadcasted_iota(jnp.int32, (keys, pairs * rows), 1)
    position = visible_to + lax.rem(lane, rows)
    key_at = lax.broadcasted_iota(jnp.int32, (keys, pairs * rows), 0)
    bias = jnp.where(key_at <= position, 0.0, -1e30)
    dk = jnp.zeros((keys, HD), jnp.float32)
    dv = jnp.zeros((keys, HD), jnp.float32)
    for base in range(0, heads, pairs):
        cols = [slice((base + j) * HD, (base + j + 1) * HD) for j in range(pairs)]
        q_g = jnp.concatenate([q[:, c] for c in cols], axis=0)
        do_g = jnp.concatenate([do[:, c] for c in cols], axis=0)
        s = dot(key_rows, q_g, NT) * (scale * math.log2(math.e)) + bias
        e = jnp.exp2(s - jnp.max(s, axis=0, keepdims=True))
        p = e * (1.0 / jnp.sum(e, axis=0, keepdims=True))
        dv = dv + dot(p.astype(jnp.bfloat16), do_g)
        dp = dot(value_rows, do_g, NT)
        delta = jnp.sum(p * dp, axis=0, keepdims=True)
        ds = (p * (dp - delta)).astype(jnp.bfloat16)
        dk = dk + dot(ds, q_g)
        dq = (dot(keys_t, ds) * scale).T.astype(jnp.bfloat16)
        for j, c in enumerate(cols):
            dq_ref[:, c] = dq[j * rows : (j + 1) * rows]
    running[:keys, :HD] += dk * scale
    running[:keys, HD:] += dv


def stage(early, lo, hi, first, last, *refs):
    refs = list(refs)
    block_ref, q_ref, do_ref = refs[:3]
    del refs[:3]
    if early:
        top_ref, flag_ref = refs[:2]
        del refs[:2]
    kv_ref, run_in, wq_hbm, wkv_hbm = refs[:4]
    del refs[:4]
    part_out = refs.pop(0)
    run_out = refs.pop(0)
    wq, wkv, running, carry, dq_ref, part, w_sem, part_sem, run_sem = refs
    tp = lax.axis_index("tp")
    shards = [tp ^ 1, tp, tp ^ 3, tp ^ 2] if not early else [tp ^ 3, tp ^ 2, tp ^ 1, tp]
    own_slot = 1 if not early else 3
    rows = hi - lo
    copies = []
    for i, shard in enumerate(shards):
        at = pl.ds(pl.multiple_of(shard * WIDTH, WIDTH), WIDTH)
        copies.append(
            (
                pltpu.make_async_copy(wq_hbm.at[0, at], wq.at[i], w_sem.at[i, 0]),
                pltpu.make_async_copy(wkv_hbm.at[0, at], wkv.at[i], w_sem.at[i, 1]),
            )
        )
    if first:
        run_copy = pltpu.make_async_copy(run_in.at[0], carry, run_sem.at[0])
    else:
        run_copy = pltpu.make_async_copy(run_in, running, run_sem.at[0])
    run_copy.start()
    for pair in copies:
        for copy in pair:
            copy.start()
    block = block_ref[0] + (0 if early else 1)
    first_row = block * BLOCK
    keys = (BLOCK if early else 2 * BLOCK) + hi
    q = q_ref[0, 0]
    if early:
        do = jnp.where(flag_ref[0] == 1, top_ref[...], do_ref[...])
    else:
        do = do_ref[0]
    run_copy.wait()
    if first:
        running[...] = carry[...].astype(jnp.float32)
    attend(q, do, kv_ref.at[0], first_row + lo, keys, dq_ref, BLOCK // rows, running)
    if last:
        below = lax.broadcasted_iota(jnp.int32, running.shape, 0) < first_row
        carry[...] = jnp.where(below, running[...], 0.0).astype(jnp.bfloat16)
        out_copy = pltpu.make_async_copy(carry, run_out.at[0], run_sem.at[1])
    else:
        out_copy = pltpu.make_async_copy(running, run_out, run_sem.at[1])
    out_copy.start()
    own = running[pl.ds(pl.multiple_of(first_row + lo, 64), rows), :].astype(jnp.bfloat16)
    dq = dq_ref[...]
    outs = []
    for i in range(4):
        for copy in copies[i]:
            copy.wait()
        total = dot(dq, wq[i], NT) + dot(own, wkv[i], NT)
        if i == own_slot:
            total = total + do.astype(jnp.float32)
        part[i] = total.astype(jnp.bfloat16)
        copy = pltpu.make_async_copy(part.at[i], part_out.at[i], part_sem.at[i])
        copy.start()
        outs.append(copy)
    for copy in outs:
        copy.wait()
    out_copy.wait()


def run_stage(early, lo, hi, first, last, block, query, do, top, flag, keyval, run, wq, wkv):
    rows = hi - lo
    row_block = lo // rows
    smem = pl.BlockSpec(memory_space=pltpu.SMEM)
    hbm = pl.BlockSpec(memory_space=pl.ANY)
    length = keyval.shape[1]
    in_specs = [
        smem,
        pl.BlockSpec((1, 1, rows, WIDTH), lambda i: (0, 1 if early else 0, row_block, 0)),
    ]
    args = [block, query, do]
    if early:
        in_specs += [
            pl.BlockSpec((rows, WIDTH), lambda i: (0, 0)),
            pl.BlockSpec((rows, WIDTH), lambda i: (row_block, 0)),
            smem,
        ]
        args += [top, flag]
    else:
        in_specs += [pl.BlockSpec((1, rows, WIDTH), lambda i: (0, row_block, 0))]
    in_specs += [
        pl.BlockSpec((1, length, KV_WIDTH), lambda i: (0, 0, 0)),
        hbm,
        hbm,
        hbm,
    ]
    args += [keyval, run, wq, wkv]
    if last:
        run_shape = jax.ShapeDtypeStruct((1, length, KV_WIDTH), jnp.bfloat16)
    else:
        run_shape = jax.ShapeDtypeStruct((length, KV_WIDTH), jnp.float32)
    return pl.pallas_call(
        functools.partial(stage, early, lo, hi, first, last),
        grid=(1,),
        out_shape=(jax.ShapeDtypeStruct((4, rows, WIDTH), jnp.bfloat16), run_shape),
        in_specs=in_specs,
        out_specs=(hbm, hbm),
        scratch_shapes=[
            pltpu.VMEM((4, WIDTH, WIDTH), jnp.bfloat16),
            pltpu.VMEM((4, WIDTH, KV_WIDTH), jnp.bfloat16),
            pltpu.VMEM((length, KV_WIDTH), jnp.float32),
            pltpu.VMEM((length, KV_WIDTH), jnp.bfloat16),
            pltpu.VMEM((rows, WIDTH), jnp.bfloat16),
            pltpu.VMEM((4, rows, WIDTH), jnp.bfloat16),
            pltpu.SemaphoreType.DMA((4, 2)),
            pltpu.SemaphoreType.DMA((4,)),
            pltpu.SemaphoreType.DMA((2,)),
        ],
        compiler_params=pltpu.CompilerParams(vmem_limit_bytes=48 * 1024 * 1024),
        cost_estimate=pl.CostEstimate(
            flops=2 * rows * 1280 * 4096 + 20 * 8 * rows * 640 * HD,
            bytes_accessed=13 * 1024 * 1024,
            transcendentals=0,
        ),
        name=("early" if early else "late") + str(lo),
    )(*args)


def swap(block, mask):
    return lax.ppermute(block, "tp", [(i, i ^ mask) for i in range(lax.axis_size("tp"))])


def shift_down(block):
    sections, tp = lax.axis_size("section"), lax.axis_size("tp")
    route = [
        (s * tp + t, (s - 1) * tp + (t ^ 2)) for s in range(1, sections) for t in range(tp)
    ]
    return lax.ppermute(block, ("section", "tp"), route)


def total_of(*terms):
    out = terms[0].astype(jnp.float32)
    for term in terms[1:]:
        out = out + term.astype(jnp.float32)
    return out.astype(jnp.bfloat16)


def local(query, keyval, q_weight, kv_weight, block_index, carry_in, grad_late, grad_top):
    run = carry_in
    shifted = []
    for n, (lo, hi) in enumerate(CHUNKS):
        part, run = run_stage(
            False, lo, hi, n == 0, False, block_index, query, grad_late, None, None,
            keyval, run, q_weight, kv_weight,
        )
        ahead = total_of(part[1], swap(part[0], 1))
        rest = (part[3], swap(part[2], 1))
        shifted.append(shift_down(total_of(*rest, swap(ahead, 2))))
    is_last = lax.axis_index("section") == lax.axis_size("section") - 1
    flag = is_last.astype(jnp.int32).reshape(1)
    outs = {}
    for n, (lo, hi) in enumerate(CHUNKS):
        last = n == len(CHUNKS) - 1
        part, run = run_stage(
            True, lo, hi, False, last, block_index, query, shifted[n], grad_top, flag,
            keyval, run, q_weight, kv_weight,
        )
        ahead = total_of(part[1], swap(part[0], 1))
        rest = (part[3], swap(part[2], 1))
        outs[lo] = total_of(*rest, swap(ahead, 2))
    early_dx = jnp.concatenate([outs[lo] for lo in sorted(outs)], axis=0)
    return (early_dx[None], run)


def solution(mesh):
    in_specs = (
        P("section", None, None, "tp"),
        P("section", None, "tp"),
        P("section", None, "tp"),
        P("section", None, "tp"),
        P("section"),
        P("section", None, "tp"),
        P("section", None, "tp"),
        P(None, "tp"),
    )
    out_specs = (P("section", None, "tp"), P("section", None, "tp"))
    return jax.shard_map(local, mesh=mesh, in_specs=in_specs, out_specs=out_specs, check_vma=False)
```

time: 229 us -> 87.8 us (0.38)
  the two profiles are of different devices: /device:TPU:1 before, /device:TPU:6 now
where the time goes in v1:
time: 87.8 us; the launch traced here: 87.4 us
  Pallas kernels  34.6 us (39%)
  starting transfers between devices  21.5 us (24%)
  waiting for transfers between devices  18.2 us (21%)
  local copies, waits for them, and re-layouts  7.36 us (8%)
  other arithmetic  4.11 us (5%)
  between operations  1.54 us (2%)
    pallas_call x4, Pallas kernels, run_stage(): pl.pallas_call(functools.partial(stage, early, lo, hi, first, last), grid...  34.6 us
    ppermute x12, waiting for transfers between devices, swap(): lax.ppermute(block, 'tp', [(i, i ^ mask) for i in range(lax.axis_size('tp...  18.2 us
    ppermute x2, starting transfers between devices, shift_down(): return lax.ppermute(block, ('section', 'tp'), route)  15.1 us
    unnamed x22, local copies, waits for them, and re-layouts  6.45 us
    ppermute x12, starting transfers between devices, swap(): lax.ppermute(block, 'tp', [(i, i ^ mask) for i in range(lax.axis_size('tp...  6.36 us
    convert_element_type x8, other arithmetic, total_of(): return out.astype(jnp.bfloat16)  3.29 us
  transfers between devices with their start and end apart: 14, of which 4 were waited for; matrix products, arithmetic and copies ran while one was open for 5% of the time, Pallas kernels for 20%

profile of v1, /device:TPU:6, one launch (start us, length us, event | category | flops | bytes accessed | tf_op | source)
XLA Modules:
  0.0 87.4 jit_solution(15104220256690075919)
XLA Ops:
  1.3 0.0 copy-start.1
  1.3 1.2 %copy-done.1 = bf16[1,2,256,1024]{3,2,1,0:T(8,128)(2,1)S(1)} copy-done((bf16[1,2,256,1024]{3,2,1,0:T(8,128)(2,1)S(1)}, bf16[1,2,256,1024]{3,2,1,0:T(8,128)(2,1)}, u32[]{:S(2)}) %copy-start.1) | copy-done | bytes 1048600
  2.5 1.0 %copy-done.3 = bf16[1,768,256]{2,1,0:T(8,128)(2,1)S(1)} copy-done((bf16[1,768,256]{2,1,0:T(8,128)(2,1)S(1)}, bf16[1,768,256]{2,1,0:T(8,128)(2,1)}, u32[]{:S(2)}) %copy-start.3) | copy-done | bytes 393240
  3.5 1.0 %copy-done.5 = bf16[1,256,1024]{2,1,0:T(8,128)(2,1)S(1)} copy-done((bf16[1,256,1024]{2,1,0:T(8,128)(2,1)S(1)}, bf16[1,256,1024]{2,1,0:T(8,128)(2,1)}, u32[]{:S(2)}) %copy-start.5) | copy-done | bytes 524312
  4.5 1.0 %copy-done.10 = bf16[1,768,256]{2,1,0:T(8,128)(2,1)S(1)} copy-done((bf16[1,768,256]{2,1,0:T(8,128)(2,1)S(1)}, bf16[1,768,256]{2,1,0:T(8,128)(2,1)}, u32[]{:S(2)}) %copy-start.10) | copy-done | bytes 393240
  5.5 8.2 %late128.1 = (bf16[4,128,1024]{2,1,0:T(8,128)(2,1)S(1)}, f32[768,256]{1,0:T(8,128)S(1)}) custom-call(s32[1]{0:T(128)S(6)} %copy.10.refs_0_, bf16[1,2,256,1024]{3,2,1,0:T(8,128)(2,1)S(1)} %copy-done.1, bf16[1,256,1024]{2,1,0:T(8,128)(2,1)S(1)} %copy-done.5, bf16[1,768,256]{2,1,0:T(8,128)(2,1)S(1)} %copy-done.3, bf16[1,768,256]{2,1,0:T(8,128)(2,1)S(1)} %copy-done.10, ...), custom_call_target="tpu_custom_call" | custom-call | flops 3019898880 | bytes 13631488 | tf_op jit(solution)/shard_map/late128/pallas_call | solution.py:157
  13.8 0.3 collective-permute-start.5
  14.1 0.0 copy-start.2
  14.1 0.0 copy-start.4
  14.1 9.6 %late0.1 = (bf16[4,128,1024]{2,1,0:T(8,128)(2,1)S(1)}, f32[768,256]{1,0:T(8,128)S(1)}) custom-call(s32[1]{0:T(128)S(6)} %copy.10.refs_0_, bf16[1,2,256,1024]{3,2,1,0:T(8,128)(2,1)S(1)} %copy-done.1, bf16[1,256,1024]{2,1,0:T(8,128)(2,1)S(1)} %copy-done.5, bf16[1,768,256]{2,1,0:T(8,128)(2,1)S(1)} %copy-done.3, f32[768,256]{1,0:T(8,128)S(1)} %get-tuple-element.10.refs_4_, ...), custom_call_target="tpu_custom_call" | custom-call | flops 3019898880 | bytes 13631488 | tf_op jit(solution)/shard_map/late0/pallas_call | solution.py:157
  23.7 0.8 slice_bitcast_fusion.7
  24.5 0.5 collective-permute-start.1
  24.9 0.1 collective-permute-start.4
  25.0 0.1 fusion.6
  25.1 0.0 copy-start
  25.1 1.7 %collective-permute-start.6 = (bf16[128,1024]{1,0:T(8,128)(2,1)S(1)}, bf16[128,1024]{1,0:T(8,128)(2,1)S(1)}, u32[]{:S(2)}, u32[]{:S(2)}) collective-permute-start(bf16[128,1024]{1,0:T(8,128)(2,1)S(1)} %fusion.6), channel_id=1, source_target_pairs={{0,2},{1,3},{2,0},{3,1},{4,6},{5,7},{6,4},{7,5},{8,10},{9,11},{10,... | collective-permute-start | bytes 786440 | tf_op jit(solution)/shard_map/ppermute | solution.py:185
  26.7 0.2 collective-permute-start
  26.9 0.8 fusion.9
  27.7 0.8 collective-permute-start.2
  28.5 0.0 collective-permute-done.4
  28.5 5.8 %collective-permute-done.6 = bf16[128,1024]{1,0:T(8,128)(2,1)S(1)} collective-permute-done((bf16[128,1024]{1,0:T(8,128)(2,1)S(1)}, bf16[128,1024]{1,0:T(8,128)(2,1)S(1)}, u32[]{:S(2)}, u32[]{:S(2)}) %collective-permute-start.6) | collective-permute-done | bytes 262176 | tf_op jit(solution)/shard_map/ppermute | solution.py:185
  34.3 0.8 fusion.8
  35.1 10.5 %collective-permute-start.7 = (bf16[128,1024]{1,0:T(8,128)(2,1)}, bf16[128,1024]{1,0:T(8,128)(2,1)}, u32[]{:S(2)}, u32[]{:S(2)}) collective-permute-start(bf16[128,1024]{1,0:T(8,128)(2,1)} %fusion.8), channel_id=1, source_target_pairs={{4,2},{5,3},{6,0},{7,1},{8,6},{9,7},{10,4},{11,5},{12,10},{13,11},... | collective-permute-start | bytes 786440 | tf_op jit(solution)/shard_map/ppermute | solution.py:193
  45.6 0.0 collective-permute-done.2
  45.6 1.2 %fusion.11 = bf16[128,1024]{1,0:T(8,128)(2,1)S(1)} fusion(bf16[128,1024]{1,0:T(8,128)(2,1)} %collective-permute-done.2, bf16[128,1024]{1,0:T(8,128)(2,1)} %collective-permute-done, bf16[4,128,1024]{2,1,0:T(8,128)(2,1)} %copy-done.7), kind=kLoop, calls=%fused_computation.20 | loop fusion | flops 786432 | bytes 1048576 | tf_op jit(solution)/shard_map/convert_element_type | solution.py:200
  46.9 4.7 %collective-permute-start.3 = (bf16[128,1024]{1,0:T(8,128)(2,1)S(1)}, bf16[128,1024]{1,0:T(8,128)(2,1)S(1)}, u32[]{:S(2)}, u32[]{:S(2)}) collective-permute-start(bf16[128,1024]{1,0:T(8,128)(2,1)S(1)} %fusion.11), channel_id=1, source_target_pairs={{4,2},{5,3},{6,0},{7,1},{8,6},{9,7},{10,4},{11,5},{12,10},{13,11},... | collective-permute-start | bytes 786440 | tf_op jit(solution)/shard_map/ppermute | solution.py:193
  51.5 0.0 collective-permute-done.7.refs_2_
  51.5 0.0 copy-start.6
  51.6 1.0 %copy-done.6 = bf16[256,1024]{1,0:T(8,128)(2,1)S(1)} copy-done((bf16[256,1024]{1,0:T(8,128)(2,1)S(1)}, bf16[256,1024]{1,0:T(8,128)(2,1)}, u32[]{:S(2)}) %copy-start.6) | copy-done | bytes 524312
  52.6 1.1 %copy-done.9 = f32[768,256]{1,0:T(8,128)S(1)} copy-done((f32[768,256]{1,0:T(8,128)S(1)}, f32[768,256]{1,0:T(8,128)}, u32[]{:S(2)}) %copy-start.9) | copy-done | bytes 786456
  53.7 8.0 %early128.1 = (bf16[4,128,1024]{2,1,0:T(8,128)(2,1)S(1)}, f32[768,256]{1,0:T(8,128)S(1)}) custom-call(s32[1]{0:T(128)S(6)} %copy.10.refs_0_, bf16[1,2,256,1024]{3,2,1,0:T(8,128)(2,1)S(1)} %copy-done.2, bf16[128,1024]{1,0:T(8,128)(2,1)} %collective-permute-done.7.refs_2_, bf16[256,1024]{1,0:T(8,128)(2,1)S(1)} %copy-done.6, s32[1]{0:T(128)} %bitcast.4.refs_4_, ...), custom_call_target="tpu_custom_call" | custom-call | flops 3019898880 | bytes 13631488 | tf_op jit(solution)/shard_map/early128/pallas_call | solution.py:157
  61.7 8.9 %early0.1 = (bf16[4,128,1024]{2,1,0:T(8,128)(2,1)S(1)}, bf16[1,768,256]{2,1,0:T(8,128)(2,1)}) custom-call(s32[1]{0:T(128)S(6)} %copy.10.refs_0_, bf16[1,2,256,1024]{3,2,1,0:T(8,128)(2,1)S(1)} %copy-done.2, bf16[128,1024]{1,0:T(8,128)(2,1)S(1)} %collective-permute-done.3.refs_2_, bf16[256,1024]{1,0:T(8,128)(2,1)S(1)} %copy-done.6, s32[1]{0:T(128)} %bitcast.4.refs_4_, ...), custom_call_target="tpu_custom_call" | custom-call | flops 3019898880 | bytes 13631488 | tf_op jit(solution)/shard_map/early0/pallas_call | solution.py:157
  70.7 0.1 collective-permute-start.9
  70.8 0.6 collective-permute-start.12
  71.4 0.1 collective-permute-start.8
  71.5 0.8 collective-permute-done.9
  72.3 0.1 fusion.3
  72.4 0.2 collective-permute-start.10
  72.6 0.1 collective-permute-start.11
  72.7 0.0 collective-permute-done.12
  72.7 0.1 fusion
  72.8 1.9 %collective-permute-start.13 = (bf16[128,1024]{1,0:T(8,128)(2,1)S(1)}, bf16[128,1024]{1,0:T(8,128)(2,1)S(1)}, u32[]{:S(2)}, u32[]{:S(2)}) collective-permute-start(bf16[128,1024]{1,0:T(8,128)(2,1)S(1)} %fusion), channel_id=1, source_target_pairs={{0,2},{1,3},{2,0},{3,1},{4,6},{5,7},{6,4},{7,5},{8,10},{9,11},{10,... | collective-permute-start | bytes 786440 | tf_op jit(solution)/shard_map/ppermute | solution.py:185
  74.6 0.0 collective-permute-done.8
  74.6 7.0 %collective-permute-done.10 = bf16[128,1024]{1,0:T(8,128)(2,1)S(1)} collective-permute-done((bf16[128,1024]{1,0:T(8,128)(2,1)S(1)}, bf16[128,1024]{1,0:T(8,128)(2,1)S(1)}, u32[]{:S(2)}, u32[]{:S(2)}) %collective-permute-start.10) | collective-permute-done | bytes 262176 | tf_op jit(solution)/shard_map/ppermute | solution.py:185
  81.6 0.1 fusion.5
  81.7 4.7 %collective-permute-done.13 = bf16[128,1024]{1,0:T(8,128)(2,1)S(1)} collective-permute-done((bf16[128,1024]{1,0:T(8,128)(2,1)S(1)}, bf16[128,1024]{1,0:T(8,128)(2,1)S(1)}, u32[]{:S(2)}, u32[]{:S(2)}) %collective-permute-start.13) | collective-permute-done | bytes 262176 | tf_op jit(solution)/shard_map/ppermute | solution.py:185
  86.4 0.1 fusion.2
  86.5 0.8 maximum_bitcast_fusion
  (19 shorter events, 0.1 us)
Async XLA Ops:
  1.3 1.2 %copy-start.1 = (bf16[1,2,256,1024]{3,2,1,0:T(8,128)(2,1)S(1)}, bf16[1,2,256,1024]{3,2,1,0:T(8,128)(2,1)}, u32[]{:S(2)}) copy-start(bf16[1,2,256,1024]{3,2,1,0:T(8,128)(2,1)} %refs_1_.7) | copy-start | bytes 3145732
  2.5 1.0 %copy-start.3 = (bf16[1,768,256]{2,1,0:T(8,128)(2,1)S(1)}, bf16[1,768,256]{2,1,0:T(8,128)(2,1)}, u32[]{:S(2)}) copy-start(bf16[1,768,256]{2,1,0:T(8,128)(2,1)} %refs_5_.7) | copy-start | bytes 1179652
  3.5 1.0 %copy-start.5 = (bf16[1,256,1024]{2,1,0:T(8,128)(2,1)S(1)}, bf16[1,256,1024]{2,1,0:T(8,128)(2,1)}, u32[]{:S(2)}) copy-start(bf16[1,256,1024]{2,1,0:T(8,128)(2,1)} %refs_2_.3) | copy-start | bytes 1572868
  4.5 1.0 %copy-start.10 = (bf16[1,768,256]{2,1,0:T(8,128)(2,1)S(1)}, bf16[1,768,256]{2,1,0:T(8,128)(2,1)}, u32[]{:S(2)}) copy-start(bf16[1,768,256]{2,1,0:T(8,128)(2,1)} %refs_4_.1) | copy-start | bytes 1179652
  13.8 11.2 %collective-permute-start.5 = (bf16[128,1024]{1,0:T(8,128)(2,1)S(1)}, bf16[128,1024]{1,0:T(8,128)(2,1)S(1)}, u32[]{:S(2)}, u32[]{:S(2)}) collective-permute-start(bf16[128,1024]{1,0:T(8,128)(2,1)S(1)} %get-tuple-element.25), channel_id=1, source_target_pairs={{0,1},{1,0},{2,3},{3,2},{4,5},{5,4},{6,7},{7,6},{8,9},{9,8},{10,11... | collective-permute-start | bytes 786440 | tf_op jit(solution)/shard_map/ppermute | solution.py:185
  14.1 37.5 %copy-start.2 = (bf16[1,2,256,1024]{3,2,1,0:T(8,128)(2,1)S(1)}, bf16[1,2,256,1024]{3,2,1,0:T(8,128)(2,1)}, u32[]{:S(2)}) copy-start(bf16[1,2,256,1024]{3,2,1,0:T(8,128)(2,1)} %refs_1_.7) | copy-start | bytes 3145732
  14.1 37.5 %copy-start.4 = (bf16[1,768,256]{2,1,0:T(8,128)(2,1)S(1)}, bf16[1,768,256]{2,1,0:T(8,128)(2,1)}, u32[]{:S(2)}) copy-start(bf16[1,768,256]{2,1,0:T(8,128)(2,1)} %refs_5_.7) | copy-start | bytes 1179652
  23.7 3.3 %copy-start.7 = (bf16[4,128,1024]{2,1,0:T(8,128)(2,1)}, bf16[4,128,1024]{2,1,0:T(8,128)(2,1)S(1)}, u32[]{:S(2)}) copy-start(bf16[4,128,1024]{2,1,0:T(8,128)(2,1)S(1)} %get-tuple-element.11) | copy-start | bytes 3145732
  23.7 11.4 %copy-start.8 = (f32[768,256]{1,0:T(8,128)}, f32[768,256]{1,0:T(8,128)S(1)}, u32[]{:S(2)}) copy-start(f32[768,256]{1,0:T(8,128)S(1)} %get-tuple-element.13.refs_6_) | copy-start | bytes 2359300
  24.5 2.4 %collective-permute-start.1 = (bf16[128,1024]{1,0:T(8,128)(2,1)S(1)}, bf16[128,1024]{1,0:T(8,128)(2,1)S(1)}, u32[]{:S(2)}, u32[]{:S(2)}) collective-permute-start(bf16[128,1024]{1,0:T(8,128)(2,1)S(1)} %get-tuple-element.21), channel_id=1, source_target_pairs={{0,1},{1,0},{2,3},{3,2},{4,5},{5,4},{6,7},{7,6},{8,9},{9,8},{10,11... | collective-permute-start | bytes 786440 | tf_op jit(solution)/shard_map/ppermute | solution.py:185
  24.9 3.5 %collective-permute-start.4 = (bf16[128,1024]{1,0:T(8,128)(2,1)S(1)}, bf16[128,1024]{1,0:T(8,128)(2,1)S(1)}, u32[]{:S(2)}, u32[]{:S(2)}) collective-permute-start(bf16[128,1024]{1,0:T(8,128)(2,1)S(1)} %get-tuple-element.24), channel_id=1, source_target_pairs={{0,1},{1,0},{2,3},{3,2},{4,5},{5,4},{6,7},{7,6},{8,9},{9,8},{10,11... | collective-permute-start | bytes 786440 | tf_op jit(solution)/shard_map/ppermute | solution.py:185
  25.1 36.7 %copy-start = (bf16[1,4096,256]{2,1,0:T(8,128)(2,1)S(1)}, bf16[1,4096,256]{2,1,0:T(8,128)(2,1)}, u32[]{:S(2)}) copy-start(bf16[1,4096,256]{2,1,0:T(8,128)(2,1)} %refs_8_.3) | copy-start | bytes 6291460
  25.1 9.2 %collective-permute-start.6 = (bf16[128,1024]{1,0:T(8,128)(2,1)S(1)}, bf16[128,1024]{1,0:T(8,128)(2,1)S(1)}, u32[]{:S(2)}, u32[]{:S(2)}) collective-permute-start(bf16[128,1024]{1,0:T(8,128)(2,1)S(1)} %fusion.6), channel_id=1, source_target_pairs={{0,2},{1,3},{2,0},{3,1},{4,6},{5,7},{6,4},{7,5},{8,10},{9,11},{10,... | collective-permute-start | bytes 786440 | tf_op jit(solution)/shard_map/ppermute | solution.py:185
  26.7 18.9 %collective-permute-start = (bf16[128,1024]{1,0:T(8,128)(2,1)}, bf16[128,1024]{1,0:T(8,128)(2,1)}, u32[]{:S(2)}, u32[]{:S(2)}) collective-permute-start(bf16[128,1024]{1,0:T(8,128)(2,1)} %get-tuple-element.20), channel_id=1, source_target_pairs={{0,1},{1,0},{2,3},{3,2},{4,5},{5,4},{6,7},{7,6},{8,9},{9,8},{10,11... | collective-permute-start | bytes 786440 | tf_op jit(solution)/shard_map/ppermute | solution.py:185
  27.7 17.9 %collective-permute-start.2 = (bf16[128,1024]{1,0:T(8,128)(2,1)}, bf16[128,1024]{1,0:T(8,128)(2,1)}, u32[]{:S(2)}, u32[]{:S(2)}) collective-permute-start(bf16[128,1024]{1,0:T(8,128)(2,1)} %fusion.9), channel_id=1, source_target_pairs={{0,2},{1,3},{2,0},{3,1},{4,6},{5,7},{6,4},{7,5},{8,10},{9,11},{10,... | collective-permute-start | bytes 786440 | tf_op jit(solution)/shard_map/ppermute | solution.py:185
  35.1 16.4 %collective-permute-start.7 = (bf16[128,1024]{1,0:T(8,128)(2,1)}, bf16[128,1024]{1,0:T(8,128)(2,1)}, u32[]{:S(2)}, u32[]{:S(2)}) collective-permute-start(bf16[128,1024]{1,0:T(8,128)(2,1)} %fusion.8), channel_id=1, source_target_pairs={{4,2},{5,3},{6,0},{7,1},{8,6},{9,7},{10,4},{11,5},{12,10},{13,11},... | collective-permute-start | bytes 786440 | tf_op jit(solution)/shard_map/ppermute | solution.py:193
  46.9 14.9 %collective-permute-start.3 = (bf16[128,1024]{1,0:T(8,128)(2,1)S(1)}, bf16[128,1024]{1,0:T(8,128)(2,1)S(1)}, u32[]{:S(2)}, u32[]{:S(2)}) collective-permute-start(bf16[128,1024]{1,0:T(8,128)(2,1)S(1)} %fusion.11), channel_id=1, source_target_pairs={{4,2},{5,3},{6,0},{7,1},{8,6},{9,7},{10,4},{11,5},{12,10},{13,11},... | collective-permute-start | bytes 786440 | tf_op jit(solution)/shard_map/ppermute | solution.py:193
  51.5 1.0 %copy-start.6 = (bf16[256,1024]{1,0:T(8,128)(2,1)S(1)}, bf16[256,1024]{1,0:T(8,128)(2,1)}, u32[]{:S(2)}) copy-start(bf16[256,1024]{1,0:T(8,128)(2,1)} %refs_3_.7) | copy-start | bytes 1572868
  52.6 1.1 %copy-start.9 = (f32[768,256]{1,0:T(8,128)S(1)}, f32[768,256]{1,0:T(8,128)}, u32[]{:S(2)}) copy-start(f32[768,256]{1,0:T(8,128)} %copy-done.8) | copy-start | bytes 2359300
  70.7 1.6 %collective-permute-start.9 = (bf16[128,1024]{1,0:T(8,128)(2,1)S(1)}, bf16[128,1024]{1,0:T(8,128)(2,1)S(1)}, u32[]{:S(2)}, u32[]{:S(2)}) collective-permute-start(bf16[128,1024]{1,0:T(8,128)(2,1)S(1)} %get-tuple-element.19), channel_id=1, source_target_pairs={{0,1},{1,0},{2,3},{3,2},{4,5},{5,4},{6,7},{7,6},{8,9},{9,8},{10,11... | collective-permute-start | bytes 786440 | tf_op jit(solution)/shard_map/ppermute | solution.py:185
  70.8 1.9 %collective-permute-start.12 = (bf16[128,1024]{1,0:T(8,128)(2,1)S(1)}, bf16[128,1024]{1,0:T(8,128)(2,1)S(1)}, u32[]{:S(2)}, u32[]{:S(2)}) collective-permute-start(bf16[128,1024]{1,0:T(8,128)(2,1)S(1)} %get-tuple-element.23), channel_id=1, source_target_pairs={{0,1},{1,0},{2,3},{3,2},{4,5},{5,4},{6,7},{7,6},{8,9},{9,8},{10,11... | collective-permute-start | bytes 786440 | tf_op jit(solution)/shard_map/ppermute | solution.py:185
  71.4 3.3 %collective-permute-start.8 = (bf16[128,1024]{1,0:T(8,128)(2,1)S(1)}, bf16[128,1024]{1,0:T(8,128)(2,1)S(1)}, u32[]{:S(2)}, u32[]{:S(2)}) collective-permute-start(bf16[128,1024]{1,0:T(8,128)(2,1)S(1)} %get-tuple-element.18), channel_id=1, source_target_pairs={{0,1},{1,0},{2,3},{3,2},{4,5},{5,4},{6,7},{7,6},{8,9},{9,8},{10,11... | collective-permute-start | bytes 786440 | tf_op jit(solution)/shard_map/ppermute | solution.py:185
  72.4 9.2 %collective-permute-start.10 = (bf16[128,1024]{1,0:T(8,128)(2,1)S(1)}, bf16[128,1024]{1,0:T(8,128)(2,1)S(1)}, u32[]{:S(2)}, u32[]{:S(2)}) collective-permute-start(bf16[128,1024]{1,0:T(8,128)(2,1)S(1)} %fusion.3), channel_id=1, source_target_pairs={{0,2},{1,3},{2,0},{3,1},{4,6},{5,7},{6,4},{7,5},{8,10},{9,11},{10,... | collective-permute-start | bytes 786440 | tf_op jit(solution)/shard_map/ppermute | solution.py:185
  72.6 9.1 %collective-permute-start.11 = (bf16[128,1024]{1,0:T(8,128)(2,1)S(1)}, bf16[128,1024]{1,0:T(8,128)(2,1)S(1)}, u32[]{:S(2)}, u32[]{:S(2)}) collective-permute-start(bf16[128,1024]{1,0:T(8,128)(2,1)S(1)} %get-tuple-element.22), channel_id=1, source_target_pairs={{0,1},{1,0},{2,3},{3,2},{4,5},{5,4},{6,7},{7,6},{8,9},{9,8},{10,11... | collective-permute-start | bytes 786440 | tf_op jit(solution)/shard_map/ppermute | solution.py:185
  72.8 13.7 %collective-permute-start.13 = (bf16[128,1024]{1,0:T(8,128)(2,1)S(1)}, bf16[128,1024]{1,0:T(8,128)(2,1)S(1)}, u32[]{:S(2)}, u32[]{:S(2)}) collective-permute-start(bf16[128,1024]{1,0:T(8,128)(2,1)S(1)} %fusion), channel_id=1, source_target_pairs={{0,2},{1,3},{2,0},{3,1},{4,6},{5,7},{6,4},{7,5},{8,10},{9,11},{10,... | collective-permute-start | bytes 786440 | tf_op jit(solution)/shard_map/ppermute | solution.py:185

commit v2 on v0

v2 whole, which is shorter than its diff:
```python
import functools
import math

import jax
import jax.numpy as jnp
from jax import lax
from jax.experimental import pallas as pl
from jax.experimental.pallas import tpu as pltpu
from jax.sharding import PartitionSpec as P

HD = 128
BLOCK = 256
WIDTH = 1024
KV_WIDTH = 256
HALVES = ((128, 256), (0, 128))
PIECES = 4
NT = (((1,), (1,)), ((), ()))
NN = (((1,), (0,)), ((), ()))


def dot(a, b, dims=NN):
    return lax.dot_general(a, b, dims, preferred_element_type=jnp.float32)


def tall(ref, rows_at, out):
    heads = ref.shape[-1] // HD
    rows = rows_at.stop - rows_at.start
    for h in range(heads):
        out[h * rows : (h + 1) * rows] = ref[rows_at, h * HD : (h + 1) * HD]


def probabilities(key_rows, q_g, bias):
    scale = math.log2(math.e) / math.sqrt(HD)
    s = dot(key_rows, q_g, NT) * scale + bias
    e = jnp.exp2(s - jnp.max(s, axis=0, keepdims=True))
    return e * (1.0 / jnp.sum(e, axis=0, keepdims=True))


def visible_bias(keys, first_row, rows, lanes):
    position = first_row + lax.rem(lax.broadcasted_iota(jnp.int32, (keys, lanes), 1), rows)
    key_at = lax.broadcasted_iota(jnp.int32, (keys, lanes), 0)
    return jnp.where(key_at <= position, 0.0, -1e30)


def grad_scores(p, dp):
    delta = jnp.sum(p * dp, axis=0, keepdims=True)
    return (p * (dp - delta)).astype(jnp.bfloat16)


def add_terms(keys, kv_ref, q_all, do_all, p_all, ds_all, running, dq_ref, dq_rows):
    rows = dq_rows.stop - dq_rows.start
    scale = 1.0 / math.sqrt(HD)
    ds = ds_all[:keys]
    running[:keys, :HD] += dot(ds, q_all[...]) * scale
    running[:keys, HD:] += dot(p_all[:keys], do_all[...])
    keys_t = kv_ref[:keys, :HD].astype(jnp.float32).T.astype(jnp.bfloat16)
    dq = dot(keys_t, ds) * scale
    for h in range(dq.shape[1] // rows):
        piece = dq[:, h * rows : (h + 1) * rows].T
        dq_ref[dq_rows, h * HD : (h + 1) * HD] = piece.astype(jnp.bfloat16)


def start_all(copies):
    for copy in copies:
        copy.start()


def wait_all(copies):
    for copy in copies:
        copy.wait()


def project(dq, own, wq, wkv, slot):
    return dot(dq, wq[slot], NT) + dot(own, wkv[slot], NT)


def late_first(
    block_ref, q_hbm, do_hbm, kv_hbm, carry_hbm, wq_hbm, wkv_hbm,
    send_ref, keep_ref, run_hbm, dq_ref, own_ref, wq, wkv,
    run_ref, kv_ref, carry, q_ref, do_ref, q_all, do_all, p_all, ds_all, sem, w_sem,
):
    tp = lax.axis_index("tp")
    copies = [
        pltpu.make_async_copy(q_hbm.at[0, 0], q_ref, sem.at[0]),
        pltpu.make_async_copy(kv_hbm.at[0], kv_ref, sem.at[1]),
        pltpu.make_async_copy(do_hbm.at[0], do_ref, sem.at[2]),
        pltpu.make_async_copy(carry_hbm.at[0], carry, sem.at[3]),
    ]
    loads = []
    for i, shard in enumerate((tp ^ 1, tp, tp ^ 3, tp ^ 2)):
        at = pl.ds(pl.multiple_of(shard * WIDTH, WIDTH), WIDTH)
        loads.append(pltpu.make_async_copy(wq_hbm.at[0, at], wq.at[i], w_sem.at[i, 0]))
        loads.append(pltpu.make_async_copy(wkv_hbm.at[0, at], wkv.at[i], w_sem.at[i, 1]))
    start_all(copies)
    wait_all(copies)
    start_all(loads)
    first_row = (block_ref[0] + 1) * BLOCK
    keys = 3 * BLOCK
    tall(q_ref, slice(0, BLOCK), q_all)
    tall(do_ref, slice(0, BLOCK), do_all)
    run_ref[...] = carry[...].astype(jnp.float32)
    bias = visible_bias(keys, first_row, BLOCK, BLOCK)
    for h in range(WIDTH // HD):
        at = slice(h * BLOCK, (h + 1) * BLOCK)
        p = probabilities(kv_ref[:, :HD], q_all[at], bias)
        p_all[:, at] = p.astype(jnp.bfloat16)
        ds_all[:, at] = grad_scores(p, dot(kv_ref[:, HD:], do_all[at], NT))
    add_terms(
        keys, kv_ref, q_all, do_all, p_all, ds_all, run_ref, dq_ref, slice(0, BLOCK)
    )
    run_copy = pltpu.make_async_copy(run_ref, run_hbm, sem.at[4])
    run_copy.start()
    own_ref[...] = run_ref[pl.ds(pl.multiple_of(first_row, BLOCK), BLOCK), :].astype(jnp.bfloat16)
    wait_all(loads)
    dq, own = dq_ref[...], own_ref[...]
    send_ref[...] = project(dq, own, wq, wkv, 0).astype(jnp.bfloat16)
    keep = project(dq, own, wq, wkv, 1) + do_ref[...].astype(jnp.float32)
    keep_ref[...] = keep.astype(jnp.bfloat16)
    run_copy.wait()


def late_second(dq_ref, own_ref, wq, wkv, send_ref, keep_ref):
    dq, own = dq_ref[...], own_ref[...]
    send_ref[...] = project(dq, own, wq, wkv, 2).astype(jnp.bfloat16)
    keep_ref[...] = project(dq, own, wq, wkv, 3).astype(jnp.bfloat16)


def early_probabilities(
    block_ref, q_hbm, kv_hbm, p_b_hbm, p_t_hbm, p_b, p_t, q_all, kv_ref, q_ref, sem, p_sem
):
    copies = [
        pltpu.make_async_copy(q_hbm.at[0, 1], q_ref, sem.at[0]),
        pltpu.make_async_copy(kv_hbm.at[0], kv_ref, sem.at[1]),
    ]
    start_all(copies)
    wait_all(copies)
    outs = []
    for n, ((lo, hi), p_ref, out) in enumerate(zip(HALVES, (p_b, p_t), (p_b_hbm, p_t_hbm))):
        rows = hi - lo
        keys = BLOCK + hi
        tall(q_ref, slice(lo, hi), q_all)
        bias = visible_bias(keys, block_ref[0] * BLOCK + lo, rows, 2 * rows)
        for base in range(0, q_all.shape[0], 2 * rows):
            at = slice(base, base + 2 * rows)
            p = probabilities(kv_ref[:keys, :HD], q_all[at], bias)
            p_ref[:, at] = p.astype(jnp.bfloat16)
        outs.append(pltpu.make_async_copy(p_ref, out, p_sem.at[n]))
        outs[n].start()
    wait_all(outs)


def early_terms(lo, hi, flag_ref, passed, top_ref, kv_ref, q_all, p_ref, run_ref,
                do_ref, do_all, ds_all, dq_ref):
    rows = hi - lo
    keys = BLOCK + hi
    do_ref[lo:hi] = jnp.where(flag_ref[0] == 1, top_ref[...], passed)
    tall(do_ref, slice(lo, hi), do_all)
    for base in range(0, do_all.shape[0], 2 * rows):
        at = slice(base, base + 2 * rows)
        p = p_ref[:, at].astype(jnp.float32)
        ds_all[:keys, at] = grad_scores(p, dot(kv_ref[:keys, HD:], do_all[at], NT))
    add_terms(keys, kv_ref, q_all, do_all, p_ref, ds_all, run_ref, dq_ref, slice(lo, hi))


def early_top(
    flag_ref, do_in, do_more, q_hbm, top_hbm, kv_hbm, p_t_hbm, p_b_hbm, run_hbm,
    run_ref, dq_ref, do_out, kv_ref, p_b, qall_b, top_b,
    q_ref, top_ref, p_ref, q_all, do_ref, do_all, ds_all, dq_all, sem,
):
    (lo_b, hi_b), (lo, hi) = HALVES
    first = [
        pltpu.make_async_copy(top_hbm.at[lo:hi], top_ref, sem.at[0]),
        pltpu.make_async_copy(kv_hbm.at[0], kv_ref, sem.at[1]),
        pltpu.make_async_copy(p_t_hbm, p_ref, sem.at[2]),
    ]
    then = [
        pltpu.make_async_copy(q_hbm.at[0, 1], q_ref, sem.at[3]),
        pltpu.make_async_copy(run_hbm, run_ref, sem.at[4]),
    ]
    later = [
        pltpu.make_async_copy(p_b_hbm, p_b, sem.at[5]),
        pltpu.make_async_copy(top_hbm.at[lo_b:hi_b], top_b, sem.at[6]),
    ]
    start_all(first)
    start_all(then)
    passed = do_in[...].astype(jnp.float32) + do_more[...].astype(jnp.float32)
    wait_all(first)
    wait_all(then)
    start_all(later)
    tall(q_ref, slice(lo, hi), q_all)
    tall(q_ref, slice(lo_b, hi_b), qall_b)
    early_terms(lo, hi, flag_ref, passed.astype(jnp.bfloat16), top_ref, kv_ref, q_all, p_ref,
                run_ref, do_ref, do_all, ds_all, dq_all)
    dq_ref[...] = dq_all[lo:hi]
    do_out[...] = do_ref[lo:hi]
    wait_all(later)


def early_bottom(
    block_ref, flag_ref, do_in, top_ref, kv_ref, q_all, p_ref, run_in, dq_in, do_t,
    wq_hbm, wkv_hbm,
    send_ref, keep_ref, carry_ref, dq_ref, own_ref, do_ref, wq_out, wkv_out,
    wq, wkv, running, do_all, ds_all, w_sem,
):
    tp = lax.axis_index("tp")
    loads = []
    for i, shard in enumerate((tp ^ 3, tp ^ 2, tp ^ 1, tp)):
        at = pl.ds(pl.multiple_of(shard * WIDTH, WIDTH), WIDTH)
        q_to, kv_to = (wq.at[i], wkv.at[i]) if i < 2 else (wq_out.at[i - 2], wkv_out.at[i - 2])
        loads.append(pltpu.make_async_copy(wq_hbm.at[0, at], q_to, w_sem.at[i, 0]))
        loads.append(pltpu.make_async_copy(wkv_hbm.at[0, at], kv_to, w_sem.at[i, 1]))
    start_all(loads)
    lo, hi = HALVES[0]
    running[...] = run_in[...]
    dq_ref[:lo] = dq_in[...]
    do_ref[:lo] = do_t[...]
    early_terms(lo, hi, flag_ref, do_in[...], top_ref, kv_ref, q_all, p_ref, running,
                do_ref, do_all, ds_all, dq_ref)
    first_row = block_ref[0] * BLOCK
    own_ref[...] = running[pl.ds(pl.multiple_of(first_row, BLOCK), BLOCK), :].astype(jnp.bfloat16)
    below = lax.broadcasted_iota(jnp.int32, running.shape, 0) < first_row
    carry_ref[0] = jnp.where(below, running[...], 0.0).astype(jnp.bfloat16)
    dq, own = dq_ref[...], own_ref[...]
    wait_all(loads[:2])
    send_ref[...] = project(dq, own, wq, wkv, 0).astype(jnp.bfloat16)
    wait_all(loads[2:4])
    keep_ref[...] = project(dq, own, wq, wkv, 1).astype(jnp.bfloat16)
    wait_all(loads[4:])


def add_rows(*refs):
    *ins, out_ref = refs
    out_ref[...] = total_of(*(ref[...] for ref in ins))


def add_halves(a_ref, b_ref, top_ref, bottom_ref):
    half = top_ref.shape[0]
    top_ref[...] = total_of(a_ref[:half], b_ref[:half])
    bottom_ref[...] = total_of(a_ref[half:], b_ref[half:])


def early_second(dq_ref, own_ref, do_ref, wq, wkv, send_ref, keep_ref):
    dq, own = dq_ref[...], own_ref[...]
    send_ref[...] = project(dq, own, wq, wkv, 0).astype(jnp.bfloat16)
    keep = project(dq, own, wq, wkv, 1) + do_ref[...].astype(jnp.float32)
    keep_ref[...] = keep.astype(jnp.bfloat16)


def finish(keep_ref, got_ref, *refs):
    *pieces, out_ref = refs
    rows = pieces[0].shape[0]
    for i, piece in enumerate(pieces):
        at = slice(i * rows, (i + 1) * rows)
        out_ref[0, at] = total_of(keep_ref[at], got_ref[at], piece[...])


SMEM = pl.BlockSpec(memory_space=pltpu.SMEM)
HBM = pl.BlockSpec(memory_space=pltpu.HBM)
VMEM = pl.BlockSpec(memory_space=pltpu.VMEM)


def call(kernel, name, specs, args, outs, scratch, megabytes):
    args = [
        pltpu.with_memory_space_constraint(arg, pltpu.HBM) if spec is HBM else arg
        for arg, spec in zip(args, specs)
    ]
    return pl.pallas_call(
        kernel,
        out_shape=[
            pltpu.HBM(*out[:2]) if len(out) > 2 else jax.ShapeDtypeStruct(*out) for out in outs
        ],
        in_specs=specs,
        out_specs=[HBM if len(out) > 2 else VMEM for out in outs],
        scratch_shapes=scratch,
        compiler_params=pltpu.CompilerParams(vmem_limit_bytes=megabytes * 1024 * 1024),
        cost_estimate=pl.CostEstimate(
            flops=2 * 10**9, bytes_accessed=10**6, transcendentals=0
        ),
        name=name,
    )(*args)


def add(name, *terms):
    shape = terms[0].shape
    (out,) = call(
        add_rows, name, [VMEM] * len(terms), terms, [(shape, jnp.bfloat16)], [], 4
    )
    return out


def swap(block, mask):
    return lax.ppermute(block, "tp", [(i, i ^ mask) for i in range(lax.axis_size("tp"))])


def shift_down(block, mask):
    sections, tp = lax.axis_size("section"), lax.axis_size("tp")
    route = [
        (s * tp + t, (s - 1) % sections * tp + (t ^ mask))
        for s in range(sections)
        for t in range(tp)
    ]
    return lax.ppermute(block, ("section", "tp"), route)


def total_of(*terms):
    out = terms[0].astype(jnp.float32)
    for term in terms[1:]:
        out = out + term.astype(jnp.float32)
    return out.astype(jnp.bfloat16)


def local(query, keyval, q_weight, kv_weight, block_index, carry_in, grad_late, grad_top):
    is_last = lax.axis_index("section") == lax.axis_size("section") - 1
    flag = is_last.astype(jnp.int32).reshape(1)
    length = keyval.shape[1]
    half = BLOCK // 2
    tall_rows = BLOCK * WIDTH // HD
    bf16, f32 = jnp.bfloat16, jnp.float32
    block = ((BLOCK, WIDTH), bf16)
    half_block = ((half, WIDTH), bf16)
    half_tall = ((tall_rows // 2, HD), bf16)
    own_rows = ((BLOCK, KV_WIDTH), bf16)
    run_shape = ((length, KV_WIDTH), f32)
    kv_shape = ((length, KV_WIDTH), bf16)
    p_shapes = [((BLOCK + hi, tall_rows // 2), bf16) for _, hi in HALVES]
    q_load, kv_load = ((WIDTH, WIDTH), bf16), ((WIDTH, KV_WIDTH), bf16)
    several = lambda n, shape: ((n, *shape[0]), shape[1])
    send, keep, run, dq, own, wq, wkv = call(
        late_first,
        "late_first",
        [SMEM] + [HBM] * 6,
        [block_index, query, grad_late, keyval, carry_in, q_weight, kv_weight],
        [block, block, (*run_shape, HBM), block, own_rows]
        + [several(4, q_load), several(4, kv_load)],
        [
            pltpu.VMEM(*run_shape),
            pltpu.VMEM(*kv_shape),
            pltpu.VMEM(*kv_shape),
            pltpu.VMEM(*block),
            pltpu.VMEM(*block),
            pltpu.VMEM((tall_rows, HD), bf16),
            pltpu.VMEM((tall_rows, HD), bf16),
            pltpu.VMEM((length, tall_rows), bf16),
            pltpu.VMEM((length, tall_rows), bf16),
            pltpu.SemaphoreType.DMA((5,)),
            pltpu.SemaphoreType.DMA((4, 2)),
        ],
        20,
    )
    got = swap(send, 1)
    send2, keep2 = call(
        late_second, "late_second", [VMEM] * 4, [dq, own, wq, wkv], [block] * 2, [], 8
    )
    got2 = swap(send2, 1)
    mine_t, mine_b = call(
        add_halves, "add_mine", [VMEM] * 2, [keep, got], [half_block] * 2, [], 4
    )
    straight = shift_down(mine_t, 0)
    other = swap(mine_b, 2)
    crossed, kept = call(
        add_halves, "add_crossed", [VMEM] * 2, [keep2, got2], [half_block, half_block], [], 4
    )
    crossed = shift_down(crossed, 2)
    summed = shift_down(add("add_summed", kept, other), 2)
    p_b, p_t = call(
        early_probabilities,
        "early_probabilities",
        [SMEM, HBM, HBM],
        [block_index, query, keyval],
        [(*shape, HBM) for shape in p_shapes],
        [pltpu.VMEM(*shape) for shape in p_shapes]
        + [
            pltpu.VMEM(*half_tall),
            pltpu.VMEM(*kv_shape),
            pltpu.VMEM(*block),
            pltpu.SemaphoreType.DMA((2,)),
            pltpu.SemaphoreType.DMA((2,)),
        ],
        10,
    )
    run, dq_t, do_t, kv_held, p_b, qall_b, top_b = call(
        early_top,
        "early_top",
        [SMEM, VMEM, VMEM] + [HBM] * 6,
        [flag, straight, crossed, query, grad_top, keyval, p_t, p_b, run],
        [run_shape, half_block, half_block, kv_shape, p_shapes[0], half_tall, half_block],
        [
            pltpu.VMEM(*block),
            pltpu.VMEM(*half_block),
            pltpu.VMEM(*p_shapes[1]),
            pltpu.VMEM(*half_tall),
            pltpu.VMEM(*block),
            pltpu.VMEM(*half_tall),
            pltpu.VMEM(*p_shapes[0]),
            pltpu.VMEM(*block),
            pltpu.SemaphoreType.DMA((7,)),
        ],
        16,
    )
    send, keep, carry, dq, own, do, wq, wkv = call(
        early_bottom,
        "early_bottom",
        [SMEM, SMEM] + [VMEM] * 8 + [HBM] * 2,
        [block_index, flag, summed, top_b, kv_held, qall_b, p_b, run, dq_t, do_t]
        + [q_weight, kv_weight],
        [block, block, ((1, *kv_shape[0]), bf16), block, own_rows, block]
        + [several(2, q_load), several(2, kv_load)],
        [
            pltpu.VMEM(*several(2, q_load)),
            pltpu.VMEM(*several(2, kv_load)),
            pltpu.VMEM(*run_shape),
            pltpu.VMEM(*half_tall),
            pltpu.VMEM(*p_shapes[0]),
            pltpu.SemaphoreType.DMA((4, 2)),
        ],
        20,
    )
    got = swap(send, 1)
    send2, keep2 = call(
        early_second, "early_second", [VMEM] * 5, [dq, own, do, wq, wkv], [block] * 2, [], 8
    )
    got2 = swap(send2, 1)
    step = BLOCK // PIECES
    cuts = [slice(i * step, (i + 1) * step) for i in range(PIECES)]
    pieces = [swap(total_of(keep[cut], got[cut]), 2) for cut in cuts]
    (early_dx,) = call(
        finish,
        "finish",
        [VMEM] * (2 + PIECES),
        [keep2, got2, *pieces],
        [((1, BLOCK, WIDTH), bf16)],
        [],
        8,
    )
    return (early_dx, carry)


def solution(mesh):
    in_specs = (
        P("section", None, None, "tp"),
        P("section", None, "tp"),
        P("section", None, "tp"),
        P("section", None, "tp"),
        P("section"),
        P("section", None, "tp"),
        P("section", None, "tp"),
        P(None, "tp"),
    )
    out_specs = (P("section", None, "tp"), P("section", None, "tp"))
    return jax.shard_map(local, mesh=mesh, in_specs=in_specs, out_specs=out_specs, check_vma=False)
```

time: 229 us -> 67.8 us (0.30)
  waiting for transfers between devices: 134 us -> 15.7 us
  matrix products: 49.1 us -> 0 us
  Pallas kernels: 0 us -> 28.2 us
  starting transfers between devices: 1.54 us -> 22 us
  local copies, waits for them, and re-layouts: 15.9 us -> 0 us
  between operations: 14.9 us -> 1.39 us
  other arithmetic: 12.4 us -> 0.19 us
    psum x2 -> x0, waiting for transfers between devices: 125 us -> none  [tensor_total(): lax.psum(partial_sum.astype(jnp.bfloat16), 'tp').astype(jnp.float32)]
    dot_general x12 -> x0, matrix products: 36.9 us -> none  [the longest x2 13.9 us: project(): lax.dot_general(grad_query, q_local, contract_dims, preferred_element_typ...]
    pallas_call x0 -> x10, Pallas kernels: none -> 28.2 us  [call(): pl.pallas_call(kernel, out_shape=[pltpu.HBM(*out[:2]) if len(out) > 2 els...]
    ppermute x1 -> x12, starting transfers between devices: 1.46 us -> 22 us  [the longest x3 14.3 us: shift_down(): return lax.ppermute(block, ('section', 'tp'), route)]
    sub x2 -> x0, matrix products: 12.2 us -> none  [block_terms(): exponent = jnp.exp(masked - highest)]
    unnamed x27 -> x0, local copies, waits for them, and re-layouts: 8.14 us -> none
    ppermute x1 -> x12, waiting for transfers between devices: 9.04 us -> 15.7 us  [the longest x9 11.7 us: swap(): lax.ppermute(block, 'tp', [(i, i ^ mask) for i in range(lax.axis_size('tp...]
    convert_element_type x4 -> x1, other arithmetic: 6.58 us -> 0.19 us  [total_of(): return out.astype(jnp.bfloat16)]
  transfers between devices with their start and end apart: 3 -> 12, of which waited for: 3 -> 7; matrix products, arithmetic and copies ran while one was open for 6% -> 0% of each run, Pallas kernels for 0% -> 15%
where the time goes in v2:
time: 67.8 us; the launch traced here: 67.6 us
  Pallas kernels  28.2 us (42%)
  starting transfers between devices  22 us (32%)
  waiting for transfers between devices  15.7 us (23%)
  between operations  1.39 us (2%)
    pallas_call x10, Pallas kernels, call(): pl.pallas_call(kernel, out_shape=[pltpu.HBM(*out[:2]) if len(out) > 2 els...  28.2 us
    ppermute x3, starting transfers between devices, shift_down(): return lax.ppermute(block, ('section', 'tp'), route)  14.3 us
    ppermute x9, waiting for transfers between devices, swap(): lax.ppermute(block, 'tp', [(i, i ^ mask) for i in range(lax.axis_size('tp...  11.7 us
    ppermute x9, starting transfers between devices, swap(): lax.ppermute(block, 'tp', [(i, i ^ mask) for i in range(lax.axis_size('tp...  7.69 us
    ppermute x3, waiting for transfers between devices, shift_down(): return lax.ppermute(block, ('section', 'tp'), route)  3.98 us
  transfers between devices with their start and end apart: 12, of which 7 were waited for; matrix products, arithmetic and copies ran while one was open for 0% of the time, Pallas kernels for 15%

profile of v2, /device:TPU:1, one launch (start us, length us, event | category | flops | bytes accessed | tf_op | source)
XLA Modules:
  0.0 67.6 jit_solution(2653526242910750098)
XLA Ops:
  1.3 10.7 %late_first.1 = (bf16[256,1024]{1,0:T(8,128)(2,1)S(1)}, bf16[256,1024]{1,0:T(8,128)(2,1)S(1)}, f32[768,256]{1,0:T(8,128)}, bf16[256,1024]{1,0:T(8,128)(2,1)S(1)}...) custom-call(s32[1]{0:T(128)S(6)} %copy.10.block_ref, ...), custom_call_target="tpu_custom_call" | custom-call | flops 2000000000 | bytes 1000000 | tf_op jit(solution)/shard_map/late_first/pallas_call | solution.py:267
  12.0 3.3 %collective-permute-start.1 = (bf16[256,1024]{1,0:T(8,128)(2,1)S(1)}, bf16[256,1024]{1,0:T(8,128)(2,1)S(1)}, u32[]{:S(2)}, u32[]{:S(2)}) collective-permute-start(bf16[256,1024]{1,0:T(8,128)(2,1)S(1)} %get-tuple-element.42), channel_id=1, source_target_pairs={{0,1},{1,0},{2,3},{3,2},{4,5},{5,4},{6,7},{7,6},{8,9},{9,8},{10,11... | collective-permute-start | bytes 1572872 | tf_op jit(solution)/shard_map/ppermute | solution.py:292
  15.3 1.5 %late_second.1 = (bf16[256,1024]{1,0:T(8,128)(2,1)S(1)}, bf16[256,1024]{1,0:T(8,128)(2,1)S(1)}) custom-call(bf16[256,1024]{1,0:T(8,128)(2,1)S(1)} %get-tuple-element.34.dq_ref, bf16[256,256]{1,0:T(8,128)(2,1)S(1)} %get-tuple-element.35.own_ref, bf16[4,1024,1024]{2,1,0:T(8,128)(2,1)S(1)} %get-tuple-element.36.wq, bf16[4,1024,256]{2,1,0:T(8,128)(2,1)S(1)} %get-tuple-element.37.wkv), custom_call_target="tpu_custom_call" | custom-call | flops 2000000000 | bytes 1000000 | tf_op jit(solution)/shard_map/late_second/pallas_call | solution.py:267
  16.9 0.1 collective-permute-start
  17.0 0.0 collective-permute-done.1.b_ref
  17.0 0.1 add_mine.1
  17.1 0.1 collective-permute-start.2
  17.2 1.7 %collective-permute-done.b_ref = bf16[256,1024]{1,0:T(8,128)(2,1)S(1)} collective-permute-done((bf16[256,1024]{1,0:T(8,128)(2,1)S(1)}, bf16[256,1024]{1,0:T(8,128)(2,1)S(1)}, u32[]{:S(2)}, u32[]{:S(2)}) %collective-permute-start) | collective-permute-done | bytes 524320 | tf_op jit(solution)/shard_map/ppermute | solution.py:292
  18.9 0.1 add_crossed.1
  19.0 8.6 %collective-permute-start.5 = (bf16[128,1024]{1,0:T(8,128)(2,1)S(1)}, bf16[128,1024]{1,0:T(8,128)(2,1)S(1)}, u32[]{:S(2)}, u32[]{:S(2)}) collective-permute-start(bf16[128,1024]{1,0:T(8,128)(2,1)S(1)} %get-tuple-element.45), channel_id=1, source_target_pairs={{0,254},{1,255},{2,252},{3,253},{4,2},{5,3},{6,0},{7,1},{8,6},{9,7... | collective-permute-start | bytes 786440 | tf_op jit(solution)/shard_map/ppermute | solution.py:302
  27.5 0.3 collective-permute-start.4
  27.9 0.0 collective-permute-done.2.refs_1_
  27.9 0.1 add_summed.1
  28.0 5.4 %collective-permute-start.3 = (bf16[128,1024]{1,0:T(8,128)(2,1)S(1)}, bf16[128,1024]{1,0:T(8,128)(2,1)S(1)}, u32[]{:S(2)}, u32[]{:S(2)}) collective-permute-start(bf16[128,1024]{1,0:T(8,128)(2,1)S(1)} %add_summed.1), channel_id=1, source_target_pairs={{0,254},{1,255},{2,252},{3,253},{4,2},{5,3},{6,0},{7,1},{8,6},{9,7... | collective-permute-start | bytes 786440 | tf_op jit(solution)/shard_map/ppermute | solution.py:302
  33.4 3.8 %early_probabilities.1 = (bf16[512,1024]{1,0:T(8,128)(2,1)}, bf16[384,1024]{1,0:T(8,128)(2,1)}) custom-call(s32[1]{0:T(128)S(6)} %copy.10.block_ref, bf16[1,2,256,1024]{3,2,1,0:T(8,128)(2,1)} %q_hbm.5, bf16[1,768,256]{2,1,0:T(8,128)(2,1)} %kv_hbm.5), custom_call_target="tpu_custom_call" | custom-call | flops 2000000000 | bytes 1000000 | tf_op jit(solution)/shard_map/early_probabilities/pallas_call | solution.py:267
  37.2 0.0 collective-permute-done.5.do_more
  37.2 1.5 %collective-permute-done.4.do_in = bf16[128,1024]{1,0:T(8,128)(2,1)S(1)} collective-permute-done((bf16[128,1024]{1,0:T(8,128)(2,1)S(1)}, bf16[128,1024]{1,0:T(8,128)(2,1)S(1)}, u32[]{:S(2)}, u32[]{:S(2)}) %collective-permute-start.4) | collective-permute-done | bytes 262176 | tf_op jit(solution)/shard_map/ppermute | solution.py:302
  38.7 3.1 %early_top.1 = (f32[768,256]{1,0:T(8,128)S(1)}, bf16[128,1024]{1,0:T(8,128)(2,1)S(1)}, bf16[128,1024]{1,0:T(8,128)(2,1)S(1)}, bf16[768,256]{1,0:T(8,128)(2,1)S(1...) custom-call(s32[1]{0:T(128)} %bitcast.flag_ref, ...), custom_call_target="tpu_custom_call" | custom-call | flops 2000000000 | bytes 1000000 | tf_op jit(solution)/shard_map/early_top/pallas_call | solution.py:267
  41.9 2.5 %collective-permute-done.3.do_in = bf16[128,1024]{1,0:T(8,128)(2,1)S(1)} collective-permute-done((bf16[128,1024]{1,0:T(8,128)(2,1)S(1)}, bf16[128,1024]{1,0:T(8,128)(2,1)S(1)}, u32[]{:S(2)}, u32[]{:S(2)}) %collective-permute-start.3) | collective-permute-done | bytes 262176 | tf_op jit(solution)/shard_map/ppermute | solution.py:302
  44.3 6.2 %early_bottom.1 = (bf16[256,1024]{1,0:T(8,128)(2,1)S(1)}, bf16[256,1024]{1,0:T(8,128)(2,1)S(1)}, bf16[1,768,256]{2,1,0:T(8,128)(2,1)}, bf16[256,1024]{1,0:T(8,12...) custom-call(s32[1]{0:T(128)S(6)} %copy.10.block_ref, ...), custom_call_target="tpu_custom_call" | custom-call | flops 2000000000 | bytes 1000000 | tf_op jit(solution)/shard_map/early_bottom/pallas_call | solution.py:267
  50.6 1.0 %collective-permute-start.7 = (bf16[256,1024]{1,0:T(8,128)(2,1)S(1)}, bf16[256,1024]{1,0:T(8,128)(2,1)S(1)}, u32[]{:S(2)}, u32[]{:S(2)}) collective-permute-start(bf16[256,1024]{1,0:T(8,128)(2,1)S(1)} %get-tuple-element.64), channel_id=1, source_target_pairs={{0,1},{1,0},{2,3},{3,2},{4,5},{5,4},{6,7},{7,6},{8,9},{9,8},{10,11... | collective-permute-start | bytes 1572872 | tf_op jit(solution)/shard_map/ppermute | solution.py:292
  51.6 1.6 %early_second.1 = (bf16[256,1024]{1,0:T(8,128)(2,1)S(1)}, bf16[256,1024]{1,0:T(8,128)(2,1)S(1)}) custom-call(bf16[256,1024]{1,0:T(8,128)(2,1)S(1)} %get-tuple-element.56.dq_ref, bf16[256,256]{1,0:T(8,128)(2,1)S(1)} %get-tuple-element.57.own_ref, bf16[256,1024]{1,0:T(8,128)(2,1)S(1)} %get-tuple-element.58.do_ref, ...), custom_call_target="tpu_custom_call" | custom-call | flops 2000000000 | bytes 1000000 | tf_op jit(solution)/shard_map/early_second/pallas_call | solution.py:267
  53.2 0.1 collective-permute-start.6
  53.3 0.0 collective-permute-done.7
  53.3 0.2 add_convert_fusion
  53.5 1.0 %collective-permute-start.10 = (bf16[64,1024]{1,0:T(8,128)(2,1)S(1)}, bf16[64,1024]{1,0:T(8,128)(2,1)S(1)}, u32[]{:S(2)}, u32[]{:S(2)}) collective-permute-start(bf16[64,1024]{1,0:T(8,128)(2,1)S(1)} %get-tuple-element.67), channel_id=1, source_target_pairs={{0,2},{1,3},{2,0},{3,1},{4,6},{5,7},{6,4},{7,5},{8,10},{9,11},{10,... | collective-permute-start | bytes 393224 | tf_op jit(solution)/shard_map/ppermute | solution.py:292
  54.5 0.6 collective-permute-start.11
  55.0 0.9 %collective-permute-start.8 = (bf16[64,1024]{1,0:T(8,128)(2,1)S(1)}, bf16[64,1024]{1,0:T(8,128)(2,1)S(1)}, u32[]{:S(2)}, u32[]{:S(2)}) collective-permute-start(bf16[64,1024]{1,0:T(8,128)(2,1)S(1)} %get-tuple-element.69), channel_id=1, source_target_pairs={{0,2},{1,3},{2,0},{3,1},{4,6},{5,7},{6,4},{7,5},{8,10},{9,11},{10,... | collective-permute-start | bytes 393224 | tf_op jit(solution)/shard_map/ppermute | solution.py:292
  55.9 0.6 collective-permute-start.9
  56.5 0.0 collective-permute-done.6.got_ref
  56.5 1.6 %collective-permute-done.10.refs_2_ = bf16[64,1024]{1,0:T(8,128)(2,1)S(1)} collective-permute-done((bf16[64,1024]{1,0:T(8,128)(2,1)S(1)}, bf16[64,1024]{1,0:T(8,128)(2,1)S(1)}, u32[]{:S(2)}, u32[]{:S(2)}) %collective-permute-start.10) | collective-permute-done | bytes 131104 | tf_op jit(solution)/shard_map/ppermute | solution.py:292
  58.1 2.8 %collective-permute-done.11.refs_3_ = bf16[64,1024]{1,0:T(8,128)(2,1)S(1)} collective-permute-done((bf16[64,1024]{1,0:T(8,128)(2,1)S(1)}, bf16[64,1024]{1,0:T(8,128)(2,1)S(1)}, u32[]{:S(2)}, u32[]{:S(2)}) %collective-permute-start.11) | collective-permute-done | bytes 131104 | tf_op jit(solution)/shard_map/ppermute | solution.py:292
  61.0 2.8 %collective-permute-done.8.refs_0_ = bf16[64,1024]{1,0:T(8,128)(2,1)S(1)} collective-permute-done((bf16[64,1024]{1,0:T(8,128)(2,1)S(1)}, bf16[64,1024]{1,0:T(8,128)(2,1)S(1)}, u32[]{:S(2)}, u32[]{:S(2)}) %collective-permute-start.8) | collective-permute-done | bytes 131104 | tf_op jit(solution)/shard_map/ppermute | solution.py:292
  63.8 2.8 %collective-permute-done.9.refs_1_ = bf16[64,1024]{1,0:T(8,128)(2,1)S(1)} collective-permute-done((bf16[64,1024]{1,0:T(8,128)(2,1)S(1)}, bf16[64,1024]{1,0:T(8,128)(2,1)S(1)}, u32[]{:S(2)}, u32[]{:S(2)}) %collective-permute-start.9) | collective-permute-done | bytes 131104 | tf_op jit(solution)/shard_map/ppermute | solution.py:292
  66.6 1.0 %finish.1 = bf16[1,256,1024]{2,1,0:T(8,128)(2,1)} custom-call(bf16[256,1024]{1,0:T(8,128)(2,1)S(1)} %get-tuple-element.61.keep_ref, bf16[256,1024]{1,0:T(8,128)(2,1)S(1)} %collective-permute-done.6.got_ref, bf16[64,1024]{1,0:T(8,128)(2,1)S(1)} %collective-permute-done.8.refs_0_, bf16[64,1024]{1,0:T(8,128)(2,1)S(1)} %collective-permute-done.9.refs_1_, ...), custom_call_target="tpu_custom_call" | custom-call | flops 2000000000 | bytes 1000000 | tf_op jit(solution)/shard_map/finish/pallas_call | solution.py:267
Async XLA Ops:
  12.0 5.0 %collective-permute-start.1 = (bf16[256,1024]{1,0:T(8,128)(2,1)S(1)}, bf16[256,1024]{1,0:T(8,128)(2,1)S(1)}, u32[]{:S(2)}, u32[]{:S(2)}) collective-permute-start(bf16[256,1024]{1,0:T(8,128)(2,1)S(1)} %get-tuple-element.42), channel_id=1, source_target_pairs={{0,1},{1,0},{2,3},{3,2},{4,5},{5,4},{6,7},{7,6},{8,9},{9,8},{10,11... | collective-permute-start | bytes 1572872 | tf_op jit(solution)/shard_map/ppermute | solution.py:292
  16.9 2.0 %collective-permute-start = (bf16[256,1024]{1,0:T(8,128)(2,1)S(1)}, bf16[256,1024]{1,0:T(8,128)(2,1)S(1)}, u32[]{:S(2)}, u32[]{:S(2)}) collective-permute-start(bf16[256,1024]{1,0:T(8,128)(2,1)S(1)} %get-tuple-element.39), channel_id=1, source_target_pairs={{0,1},{1,0},{2,3},{3,2},{4,5},{5,4},{6,7},{7,6},{8,9},{9,8},{10,11... | collective-permute-start | bytes 1572872 | tf_op jit(solution)/shard_map/ppermute | solution.py:292
  17.1 10.8 %collective-permute-start.2 = (bf16[128,1024]{1,0:T(8,128)(2,1)S(1)}, bf16[128,1024]{1,0:T(8,128)(2,1)S(1)}, u32[]{:S(2)}, u32[]{:S(2)}) collective-permute-start(bf16[128,1024]{1,0:T(8,128)(2,1)S(1)} %get-tuple-element.43), channel_id=1, source_target_pairs={{0,2},{1,3},{2,0},{3,1},{4,6},{5,7},{6,4},{7,5},{8,10},{9,11},{10,... | collective-permute-start | bytes 786440 | tf_op jit(solution)/shard_map/ppermute | solution.py:292
  19.0 18.2 %collective-permute-start.5 = (bf16[128,1024]{1,0:T(8,128)(2,1)S(1)}, bf16[128,1024]{1,0:T(8,128)(2,1)S(1)}, u32[]{:S(2)}, u32[]{:S(2)}) collective-permute-start(bf16[128,1024]{1,0:T(8,128)(2,1)S(1)} %get-tuple-element.45), channel_id=1, source_target_pairs={{0,254},{1,255},{2,252},{3,253},{4,2},{5,3},{6,0},{7,1},{8,6},{9,7... | collective-permute-start | bytes 786440 | tf_op jit(solution)/shard_map/ppermute | solution.py:302
  27.5 11.2 %collective-permute-start.4 = (bf16[128,1024]{1,0:T(8,128)(2,1)S(1)}, bf16[128,1024]{1,0:T(8,128)(2,1)S(1)}, u32[]{:S(2)}, u32[]{:S(2)}) collective-permute-start(bf16[128,1024]{1,0:T(8,128)(2,1)S(1)} %get-tuple-element.44), channel_id=1, source_target_pairs={{0,252},{1,253},{2,254},{3,255},{4,0},{5,1},{6,2},{7,3},{8,4},{9,5... | collective-permute-start | bytes 786440 | tf_op jit(solution)/shard_map/ppermute | solution.py:302
  28.0 16.4 %collective-permute-start.3 = (bf16[128,1024]{1,0:T(8,128)(2,1)S(1)}, bf16[128,1024]{1,0:T(8,128)(2,1)S(1)}, u32[]{:S(2)}, u32[]{:S(2)}) collective-permute-start(bf16[128,1024]{1,0:T(8,128)(2,1)S(1)} %add_summed.1), channel_id=1, source_target_pairs={{0,254},{1,255},{2,252},{3,253},{4,2},{5,3},{6,0},{7,1},{8,6},{9,7... | collective-permute-start | bytes 786440 | tf_op jit(solution)/shard_map/ppermute | solution.py:302
  50.6 2.7 %collective-permute-start.7 = (bf16[256,1024]{1,0:T(8,128)(2,1)S(1)}, bf16[256,1024]{1,0:T(8,128)(2,1)S(1)}, u32[]{:S(2)}, u32[]{:S(2)}) collective-permute-start(bf16[256,1024]{1,0:T(8,128)(2,1)S(1)} %get-tuple-element.64), channel_id=1, source_target_pairs={{0,1},{1,0},{2,3},{3,2},{4,5},{5,4},{6,7},{7,6},{8,9},{9,8},{10,11... | collective-permute-start | bytes 1572872 | tf_op jit(solution)/shard_map/ppermute | solution.py:292
  53.2 3.3 %collective-permute-start.6 = (bf16[256,1024]{1,0:T(8,128)(2,1)S(1)}, bf16[256,1024]{1,0:T(8,128)(2,1)S(1)}, u32[]{:S(2)}, u32[]{:S(2)}) collective-permute-start(bf16[256,1024]{1,0:T(8,128)(2,1)S(1)} %get-tuple-element.62), channel_id=1, source_target_pairs={{0,1},{1,0},{2,3},{3,2},{4,5},{5,4},{6,7},{7,6},{8,9},{9,8},{10,11... | collective-permute-start | bytes 1572872 | tf_op jit(solution)/shard_map/ppermute | solution.py:292
  53.5 4.7 %collective-permute-start.10 = (bf16[64,1024]{1,0:T(8,128)(2,1)S(1)}, bf16[64,1024]{1,0:T(8,128)(2,1)S(1)}, u32[]{:S(2)}, u32[]{:S(2)}) collective-permute-start(bf16[64,1024]{1,0:T(8,128)(2,1)S(1)} %get-tuple-element.67), channel_id=1, source_target_pairs={{0,2},{1,3},{2,0},{3,1},{4,6},{5,7},{6,4},{7,5},{8,10},{9,11},{10,... | collective-permute-start | bytes 393224 | tf_op jit(solution)/shard_map/ppermute | solution.py:292
  54.5 6.5 %collective-permute-start.11 = (bf16[64,1024]{1,0:T(8,128)(2,1)S(1)}, bf16[64,1024]{1,0:T(8,128)(2,1)S(1)}, u32[]{:S(2)}, u32[]{:S(2)}) collective-permute-start(bf16[64,1024]{1,0:T(8,128)(2,1)S(1)} %get-tuple-element.66), channel_id=1, source_target_pairs={{0,2},{1,3},{2,0},{3,1},{4,6},{5,7},{6,4},{7,5},{8,10},{9,11},{10,... | collective-permute-start | bytes 393224 | tf_op jit(solution)/shard_map/ppermute | solution.py:292
  55.0 8.7 %collective-permute-start.8 = (bf16[64,1024]{1,0:T(8,128)(2,1)S(1)}, bf16[64,1024]{1,0:T(8,128)(2,1)S(1)}, u32[]{:S(2)}, u32[]{:S(2)}) collective-permute-start(bf16[64,1024]{1,0:T(8,128)(2,1)S(1)} %get-tuple-element.69), channel_id=1, source_target_pairs={{0,2},{1,3},{2,0},{3,1},{4,6},{5,7},{6,4},{7,5},{8,10},{9,11},{10,... | collective-permute-start | bytes 393224 | tf_op jit(solution)/shard_map/ppermute | solution.py:292
  55.9 10.6 %collective-permute-start.9 = (bf16[64,1024]{1,0:T(8,128)(2,1)S(1)}, bf16[64,1024]{1,0:T(8,128)(2,1)S(1)}, u32[]{:S(2)}, u32[]{:S(2)}) collective-permute-start(bf16[64,1024]{1,0:T(8,128)(2,1)S(1)} %get-tuple-element.68), channel_id=1, source_target_pairs={{0,2},{1,3},{2,0},{3,1},{4,6},{5,7},{6,4},{7,5},{8,10},{9,11},{10,... | collective-permute-start | bytes 393224 | tf_op jit(solution)/shard_map/ppermute | solution.py:292

commit v3 on v2

v3 whole, which is shorter than its diff:
```python
import functools
import math

import jax
import jax.numpy as jnp
from jax import lax
from jax.experimental import pallas as pl
from jax.experimental.pallas import tpu as pltpu
from jax.sharding import PartitionSpec as P

HD = 128
BLOCK = 256
WIDTH = 1024
KV_WIDTH = 256
HALVES = ((128, 256), (0, 128))
PIECES = 4
NT = (((1,), (1,)), ((), ()))
NN = (((1,), (0,)), ((), ()))


def dot(a, b, dims=NN):
    return lax.dot_general(a, b, dims, preferred_element_type=jnp.float32)


def tall(ref, rows_at, out):
    heads = ref.shape[-1] // HD
    rows = rows_at.stop - rows_at.start
    for h in range(heads):
        out[h * rows : (h + 1) * rows] = ref[rows_at, h * HD : (h + 1) * HD]


def probabilities(key_rows, q_g, bias):
    scale = math.log2(math.e) / math.sqrt(HD)
    s = dot(key_rows, q_g, NT) * scale + bias
    e = jnp.exp2(s - jnp.max(s, axis=0, keepdims=True))
    return e * (1.0 / jnp.sum(e, axis=0, keepdims=True))


def visible_bias(keys, first_row, rows, lanes):
    position = first_row + lax.rem(lax.broadcasted_iota(jnp.int32, (keys, lanes), 1), rows)
    key_at = lax.broadcasted_iota(jnp.int32, (keys, lanes), 0)
    return jnp.where(key_at <= position, 0.0, -1e30)


def grad_scores(p, dp):
    delta = jnp.sum(p * dp, axis=0, keepdims=True)
    return (p * (dp - delta)).astype(jnp.bfloat16)


def add_terms(keys, kv_ref, q_all, do_all, p_all, ds_all, running, dq_ref, dq_rows):
    rows = dq_rows.stop - dq_rows.start
    scale = 1.0 / math.sqrt(HD)
    ds = ds_all[:keys]
    running[:keys, :HD] += dot(ds, q_all[...]) * scale
    running[:keys, HD:] += dot(p_all[:keys], do_all[...])
    keys_t = kv_ref[:keys, :HD].astype(jnp.float32).T.astype(jnp.bfloat16)
    dq = dot(keys_t, ds) * scale
    for h in range(dq.shape[1] // rows):
        piece = dq[:, h * rows : (h + 1) * rows].T
        dq_ref[dq_rows, h * HD : (h + 1) * HD] = piece.astype(jnp.bfloat16)


def start_all(copies):
    for copy in copies:
        copy.start()


def wait_all(copies):
    for copy in copies:
        copy.wait()


def weight_loads(shards, wq_hbm, wkv_hbm, wq, wkv, sem):
    loads = []
    for i, shard in enumerate(shards):
        at = pl.ds(pl.multiple_of(shard * WIDTH, WIDTH), WIDTH)
        loads.append(pltpu.make_async_copy(wq_hbm.at[0, at], wq.at[i], sem.at[i, 0]))
        loads.append(pltpu.make_async_copy(wkv_hbm.at[0, at], wkv.at[i], sem.at[i, 1]))
    return loads


def project(dq, own, wq, wkv, slot):
    return dot(dq, wq[slot], NT) + dot(own, wkv[slot], NT)


def tall_loads(rows_of, lo, hi, out, sem):
    rows = hi - lo
    return [
        pltpu.make_async_copy(
            rows_of.at[lo:hi, h * HD : (h + 1) * HD], out.at[h * rows : (h + 1) * rows], sem.at[h]
        )
        for h in range(rows_of.shape[-1] // HD)
    ]


def wide(tall_ref, rows):
    heads = tall_ref.shape[0] // rows
    return jnp.concatenate([tall_ref[h * rows : (h + 1) * rows] for h in range(heads)], axis=1)


def late_first(
    block_ref, q_hbm, do_hbm, kv_hbm, carry_hbm, wq_hbm, wkv_hbm,
    send_ref, keep_ref, run_ref, dq_ref, own_ref, wq, wkv,
    kv_ref, carry, q_all, do_all, p_all, ds_all, sem, tall_sem, w_sem,
):
    tp = lax.axis_index("tp")
    kv_copy = pltpu.make_async_copy(kv_hbm.at[0], kv_ref, sem.at[0])
    carry_copy = pltpu.make_async_copy(carry_hbm.at[0], carry, sem.at[1])
    copies = tall_loads(q_hbm.at[0, 0], 0, BLOCK, q_all, tall_sem.at[0])
    copies += tall_loads(do_hbm.at[0], 0, BLOCK, do_all, tall_sem.at[1])
    loads = weight_loads((tp ^ 1, tp, tp ^ 3, tp ^ 2), wq_hbm, wkv_hbm, wq, wkv, w_sem)
    kv_copy.start()
    start_all(copies)
    carry_copy.start()
    first_row = (block_ref[0] + 1) * BLOCK
    keys = 3 * BLOCK
    bias = visible_bias(keys, first_row, BLOCK, BLOCK)
    kv_copy.wait()
    wait_all(copies)
    start_all(loads)
    for h in range(WIDTH // HD):
        at = slice(h * BLOCK, (h + 1) * BLOCK)
        p = probabilities(kv_ref[:, :HD], q_all[at], bias)
        p_all[:, at] = p.astype(jnp.bfloat16)
        ds_all[:, at] = grad_scores(p, dot(kv_ref[:, HD:], do_all[at], NT))
    carry_copy.wait()
    run_ref[...] = carry[...].astype(jnp.float32)
    add_terms(
        keys, kv_ref, q_all, do_all, p_all, ds_all, run_ref, dq_ref, slice(0, BLOCK)
    )
    own_ref[...] = run_ref[pl.ds(pl.multiple_of(first_row, BLOCK), BLOCK), :].astype(jnp.bfloat16)
    wait_all(loads)
    dq, own = dq_ref[...], own_ref[...]
    send_ref[...] = project(dq, own, wq, wkv, 0).astype(jnp.bfloat16)
    keep = project(dq, own, wq, wkv, 1) + wide(do_all, BLOCK).astype(jnp.float32)
    keep_ref[...] = keep.astype(jnp.bfloat16)


def late_second(dq_ref, own_ref, wq, wkv, send_ref, keep_ref):
    dq, own = dq_ref[...], own_ref[...]
    send_ref[...] = project(dq, own, wq, wkv, 2).astype(jnp.bfloat16)
    keep_ref[...] = project(dq, own, wq, wkv, 3).astype(jnp.bfloat16)


def early_probabilities(
    block_ref, q_hbm, kv_hbm, top_hbm, p_b, p_t, q_b, q_t, kv_ref, top_ref, sem, tall_sem
):
    copies = [pltpu.make_async_copy(kv_hbm.at[0], kv_ref, sem.at[0])]
    for n, ((lo, hi), q_all) in enumerate(zip(HALVES, (q_b, q_t))):
        copies += tall_loads(q_hbm.at[0, 1], lo, hi, q_all, tall_sem.at[n])
    top_copy = pltpu.make_async_copy(top_hbm, top_ref, sem.at[1])
    start_all(copies)
    top_copy.start()
    wait_all(copies)
    for (lo, hi), p_ref, q_all in zip(HALVES, (p_b, p_t), (q_b, q_t)):
        rows = hi - lo
        keys = BLOCK + hi
        bias = visible_bias(keys, block_ref[0] * BLOCK + lo, rows, 2 * rows)
        for base in range(0, q_all.shape[0], 2 * rows):
            at = slice(base, base + 2 * rows)
            p = probabilities(kv_ref[:keys, :HD], q_all[at], bias)
            p_ref[:, at] = p.astype(jnp.bfloat16)
    top_copy.wait()


def early_terms(half, passed, top_ref, kv_ref, q_all, p_ref, run_ref, do_ref, do_all, ds_all, dq_ref):
    lo, hi = half
    rows = hi - lo
    keys = BLOCK + hi
    is_last = lax.axis_index("section") == lax.axis_size("section") - 1
    do_ref[...] = jnp.where(is_last, top_ref[lo:hi], passed)
    tall(do_ref, slice(0, rows), do_all)
    for base in range(0, do_all.shape[0], 2 * rows):
        at = slice(base, base + 2 * rows)
        p = p_ref[:, at].astype(jnp.float32)
        ds_all[:keys, at] = grad_scores(p, dot(kv_ref[:keys, HD:], do_all[at], NT))
    add_terms(keys, kv_ref, q_all, do_all, p_ref, ds_all, run_ref, dq_ref, slice(0, rows))


def own_rows_of(running, first_row, rows):
    at = pl.ds(pl.multiple_of(first_row, BLOCK // 2), rows)
    return running[at, :].astype(jnp.bfloat16)


def project_all(dq, own, do_ref, wq, wkv, outs):
    for slot, out in zip((2, 3, 0, 1), outs):
        total = project(dq, own, wq, wkv, slot)
        if slot == 1:
            total = total + do_ref[...].astype(jnp.float32)
        out[...] = total.astype(jnp.bfloat16)


def early_bottom(
    block_ref, do_in, do_more, top_ref, kv_ref, q_all, p_ref, run_in, wq, wkv,
    send_ref, keep_ref, send2, keep2, run_ref,
    dq_ref, do_ref, do_all, ds_all,
):
    lo, hi = HALVES[0]
    passed = do_in[...].astype(jnp.float32) + do_more[...].astype(jnp.float32)
    run_ref[...] = run_in[...]
    early_terms(HALVES[0], passed.astype(jnp.bfloat16), top_ref, kv_ref, q_all, p_ref, run_ref,
                do_ref, do_all, ds_all, dq_ref)
    own = own_rows_of(run_ref, block_ref[0] * BLOCK + lo, hi - lo)
    project_all(dq_ref[...], own, do_ref, wq, wkv, (send_ref, keep_ref, send2, keep2))


def early_top(
    block_ref, do_in, top_ref, kv_ref, q_all, p_ref, run_in, wq, wkv,
    send_ref, keep_ref, send2, keep2, carry_ref,
    dq_ref, do_ref, running, do_all, ds_all,
):
    lo, hi = HALVES[1]
    running[...] = run_in[...]
    early_terms(HALVES[1], do_in[...], top_ref, kv_ref, q_all, p_ref, running,
                do_ref, do_all, ds_all, dq_ref)
    first_row = block_ref[0] * BLOCK
    own = own_rows_of(running, first_row + lo, hi - lo)
    project_all(dq_ref[...], own, do_ref, wq, wkv, (send_ref, keep_ref, send2, keep2))
    below = lax.broadcasted_iota(jnp.int32, running.shape, 0) < first_row
    carry_ref[0] = jnp.where(below, running[...], 0.0).astype(jnp.bfloat16)


def finish(keep_t, got_t, keep_b, got_b, *refs):
    *pieces, out_ref = refs
    rows = pieces[0].shape[0]
    half = len(pieces) // 2
    for i, piece in enumerate(pieces):
        keep, got = (keep_t, got_t) if i < half else (keep_b, got_b)
        at = slice(i % half * rows, (i % half + 1) * rows)
        out_ref[0, i * rows : (i + 1) * rows] = total_of(keep[at], got[at], piece[...])


def add_rows(*refs):
    *ins, out_ref = refs
    out_ref[...] = total_of(*(ref[...] for ref in ins))


def add_halves(a_ref, b_ref, top_ref, bottom_ref):
    half = top_ref.shape[0]
    top_ref[...] = total_of(a_ref[:half], b_ref[:half])
    bottom_ref[...] = total_of(a_ref[half:], b_ref[half:])


SMEM = pl.BlockSpec(memory_space=pltpu.SMEM)
HBM = pl.BlockSpec(memory_space=pltpu.HBM)
VMEM = pl.BlockSpec(memory_space=pltpu.VMEM)


def call(kernel, name, specs, args, outs, scratch, megabytes):
    args = [
        pltpu.with_memory_space_constraint(arg, pltpu.HBM) if spec is HBM else arg
        for arg, spec in zip(args, specs)
    ]
    return pl.pallas_call(
        kernel,
        out_shape=[
            pltpu.HBM(*out[:2]) if len(out) > 2 else jax.ShapeDtypeStruct(*out) for out in outs
        ],
        in_specs=specs,
        out_specs=[HBM if len(out) > 2 else VMEM for out in outs],
        scratch_shapes=scratch,
        compiler_params=pltpu.CompilerParams(vmem_limit_bytes=megabytes * 1024 * 1024),
        cost_estimate=pl.CostEstimate(
            flops=2 * 10**9, bytes_accessed=10**6, transcendentals=0
        ),
        name=name,
    )(*args)


def add(name, *terms):
    shape = terms[0].shape
    (out,) = call(
        add_rows, name, [VMEM] * len(terms), terms, [(shape, jnp.bfloat16)], [], 4
    )
    return out


def swap(block, mask):
    return lax.ppermute(block, "tp", [(i, i ^ mask) for i in range(lax.axis_size("tp"))])


def shift_down(block, mask):
    sections, tp = lax.axis_size("section"), lax.axis_size("tp")
    route = [
        (s * tp + t, (s - 1) % sections * tp + (t ^ mask))
        for s in range(sections)
        for t in range(tp)
    ]
    return lax.ppermute(block, ("section", "tp"), route)


def total_of(*terms):
    out = terms[0].astype(jnp.float32)
    for term in terms[1:]:
        out = out + term.astype(jnp.float32)
    return out.astype(jnp.bfloat16)


def local(query, keyval, q_weight, kv_weight, block_index, carry_in, grad_late, grad_top):
    length = keyval.shape[1]
    half = BLOCK // 2
    tall_rows = BLOCK * WIDTH // HD
    bf16, f32 = jnp.bfloat16, jnp.float32
    block = ((BLOCK, WIDTH), bf16)
    half_block = ((half, WIDTH), bf16)
    half_tall = ((tall_rows // 2, HD), bf16)
    own_rows = ((BLOCK, KV_WIDTH), bf16)
    run_shape = ((length, KV_WIDTH), f32)
    kv_shape = ((length, KV_WIDTH), bf16)
    p_shapes = [((BLOCK + hi, tall_rows // 2), bf16) for _, hi in HALVES]
    q_load, kv_load = ((WIDTH, WIDTH), bf16), ((WIDTH, KV_WIDTH), bf16)
    several = lambda n, shape: ((n, *shape[0]), shape[1])
    send, keep, run, dq, own, wq, wkv = call(
        late_first,
        "late_first",
        [SMEM] + [HBM] * 6,
        [block_index, query, grad_late, keyval, carry_in, q_weight, kv_weight],
        [block, block, run_shape, block, own_rows]
        + [several(4, q_load), several(4, kv_load)],
        [
            pltpu.VMEM(*kv_shape),
            pltpu.VMEM(*kv_shape),
            pltpu.VMEM((tall_rows, HD), bf16),
            pltpu.VMEM((tall_rows, HD), bf16),
            pltpu.VMEM((length, tall_rows), bf16),
            pltpu.VMEM((length, tall_rows), bf16),
            pltpu.SemaphoreType.DMA((2,)),
            pltpu.SemaphoreType.DMA((2, WIDTH // HD)),
            pltpu.SemaphoreType.DMA((4, 2)),
        ],
        20,
    )
    got = swap(send, 1)
    send2, keep2 = call(
        late_second, "late_second", [VMEM] * 4, [dq, own, wq, wkv], [block] * 2, [], 8
    )
    got2 = swap(send2, 1)
    mine_t, mine_b = call(
        add_halves, "add_mine", [VMEM] * 2, [keep, got], [half_block] * 2, [], 4
    )
    straight = shift_down(mine_b, 0)
    other = swap(mine_t, 2)
    kept, crossed = call(
        add_halves, "add_crossed", [VMEM] * 2, [keep2, got2], [half_block, half_block], [], 4
    )
    crossed = shift_down(crossed, 2)
    summed = shift_down(add("add_summed", kept, other), 2)
    p_b, p_t, q_b, q_t, kv_held, top_held = call(
        early_probabilities,
        "early_probabilities",
        [SMEM, HBM, HBM, HBM],
        [block_index, query, keyval, grad_top],
        [*p_shapes, half_tall, half_tall, kv_shape, block],
        [pltpu.SemaphoreType.DMA((2,)), pltpu.SemaphoreType.DMA((2, WIDTH // HD))],
        10,
    )
    half_scratch = [
        pltpu.VMEM(*half_block),
        pltpu.VMEM(*half_block),
        pltpu.VMEM(*half_tall),
        pltpu.VMEM(*p_shapes[0]),
    ]
    send_b, keep_b, send2_b, keep2_b, run = call(
        early_bottom,
        "early_bottom",
        [SMEM] + [VMEM] * 9,
        [block_index, straight, crossed, top_held, kv_held, q_b, p_b, run, wq, wkv],
        [half_block] * 4 + [run_shape],
        half_scratch,
        10,
    )
    got_b, got2_b = swap(send_b, 1), swap(send2_b, 1)
    send_t, keep_t, send2_t, keep2_t, carry = call(
        early_top,
        "early_top",
        [SMEM] + [VMEM] * 8,
        [block_index, summed, top_held, kv_held, q_t, p_t, run, wq, wkv],
        [half_block] * 4 + [((1, *kv_shape[0]), bf16)],
        half_scratch[:2] + [pltpu.VMEM(*run_shape)] + half_scratch[2:],
        10,
    )
    got_t, got2_t = swap(send_t, 1), swap(send2_t, 1)
    step = BLOCK // PIECES
    cuts = [slice(i * step, (i + 1) * step) for i in range(half // step)]
    from_b = [swap(total_of(keep_b[cut], got_b[cut]), 2) for cut in cuts]
    from_t = [swap(total_of(keep_t[cut], got_t[cut]), 2) for cut in cuts]
    (early_dx,) = call(
        finish,
        "finish",
        [VMEM] * (4 + PIECES),
        [keep2_t, got2_t, keep2_b, got2_b, *from_t, *from_b],
        [((1, BLOCK, WIDTH), bf16)],
        [],
        8,
    )
    return (early_dx, carry)


def solution(mesh):
    in_specs = (
        P("section", None, None, "tp"),
        P("section", None, "tp"),
        P("section", None, "tp"),
        P("section", None, "tp"),
        P("section"),
        P("section", None, "tp"),
        P("section", None, "tp"),
        P(None, "tp"),
    )
    out_specs = (P("section", None, "tp"), P("section", None, "tp"))
    return jax.shard_map(local, mesh=mesh, in_specs=in_specs, out_specs=out_specs, check_vma=False)
```

time: 67.8 us -> 63 us (0.929)
  Pallas kernels: 28.2 us -> 24.6 us
  waiting for transfers between devices: 15.7 us -> 13.4 us
  starting transfers between devices: 22 us -> 23.5 us
    pallas_call x10 -> x9, Pallas kernels: 28.2 us -> 24.6 us  [call(): pl.pallas_call(kernel, out_shape=[pltpu.HBM(*out[:2]) if len(out) > 2 els...]
    ppermute x3, waiting for transfers between devices: 3.98 us -> 0.8 us  [shift_down(): return lax.ppermute(block, ('section', 'tp'), route)]
    ppermute x9 -> x11, starting transfers between devices: 7.69 us -> 10.2 us  [swap(): lax.ppermute(block, 'tp', [(i, i ^ mask) for i in range(lax.axis_size('tp...]
    ppermute x3, starting transfers between devices: 14.3 us -> 13.3 us  [shift_down(): return lax.ppermute(block, ('section', 'tp'), route)]
    ppermute x9 -> x11, waiting for transfers between devices: 11.7 us -> 12.6 us  [swap(): lax.ppermute(block, 'tp', [(i, i ^ mask) for i in range(lax.axis_size('tp...]
  transfers between devices with their start and end apart: 12 -> 14, of which waited for: 7 -> 6; matrix products, arithmetic and copies ran while one was open for 0% -> 0% of each run, Pallas kernels for 15% -> 23%
where the time goes in v3:
time: 63 us; the launch traced here: 62.9 us
  Pallas kernels  24.6 us (39%)
  starting transfers between devices  23.5 us (37%)
  waiting for transfers between devices  13.4 us (21%)
  between operations  1.36 us (2%)
    pallas_call x9, Pallas kernels, call(): pl.pallas_call(kernel, out_shape=[pltpu.HBM(*out[:2]) if len(out) > 2 els...  24.6 us
    ppermute x3, starting transfers between devices, shift_down(): return lax.ppermute(block, ('section', 'tp'), route)  13.3 us
    ppermute x11, waiting for transfers between devices, swap(): lax.ppermute(block, 'tp', [(i, i ^ mask) for i in range(lax.axis_size('tp...  12.6 us
    ppermute x11, starting transfers between devices, swap(): lax.ppermute(block, 'tp', [(i, i ^ mask) for i in range(lax.axis_size('tp...  10.2 us
  transfers between devices with their start and end apart: 14, of which 6 were waited for; matrix products, arithmetic and copies ran while one was open for 0% of the time, Pallas kernels for 23%

profile of v3, /device:TPU:1, one launch (start us, length us, event | category | flops | bytes accessed | tf_op | source)
XLA Modules:
  0.0 62.9 jit_solution(2085591780194455844)
XLA Ops:
  1.3 9.2 %late_first.1 = (bf16[256,1024]{1,0:T(8,128)(2,1)S(1)}, bf16[256,1024]{1,0:T(8,128)(2,1)S(1)}, f32[768,256]{1,0:T(8,128)S(1)}, bf16[256,1024]{1,0:T(8,128)(2,1)S...) custom-call(s32[1]{0:T(128)S(6)} %copy.10.block_ref, ...), custom_call_target="tpu_custom_call" | custom-call | flops 2000000000 | bytes 1000000 | tf_op jit(solution)/shard_map/late_first/pallas_call | solution.py:254
  10.5 3.3 %collective-permute-start.1 = (bf16[256,1024]{1,0:T(8,128)(2,1)S(1)}, bf16[256,1024]{1,0:T(8,128)(2,1)S(1)}, u32[]{:S(2)}, u32[]{:S(2)}) collective-permute-start(bf16[256,1024]{1,0:T(8,128)(2,1)S(1)} %get-tuple-element.39), channel_id=1, source_target_pairs={{0,1},{1,0},{2,3},{3,2},{4,5},{5,4},{6,7},{7,6},{8,9},{9,8},{10,11... | collective-permute-start | bytes 1572872 | tf_op jit(solution)/shard_map/ppermute | solution.py:279
  13.8 1.5 %late_second.1 = (bf16[256,1024]{1,0:T(8,128)(2,1)S(1)}, bf16[256,1024]{1,0:T(8,128)(2,1)S(1)}) custom-call(bf16[256,1024]{1,0:T(8,128)(2,1)S(1)} %get-tuple-element.31.dq_ref, bf16[256,256]{1,0:T(8,128)(2,1)S(1)} %get-tuple-element.32.own_ref, bf16[4,1024,1024]{2,1,0:T(8,128)(2,1)S(1)} %get-tuple-element.33.wq, bf16[4,1024,256]{2,1,0:T(8,128)(2,1)S(1)} %get-tuple-element.34.wkv), custom_call_target="tpu_custom_call" | custom-call | flops 2000000000 | bytes 1000000 | tf_op jit(solution)/shard_map/late_second/pallas_call | solution.py:254
  15.3 0.1 collective-permute-start
  15.4 0.0 collective-permute-done.1.b_ref
  15.5 0.1 add_mine.1
  15.6 0.1 collective-permute-start.2
  15.7 9.7 %collective-permute-start.4 = (bf16[128,1024]{1,0:T(8,128)(2,1)S(1)}, bf16[128,1024]{1,0:T(8,128)(2,1)S(1)}, u32[]{:S(2)}, u32[]{:S(2)}) collective-permute-start(bf16[128,1024]{1,0:T(8,128)(2,1)S(1)} %get-tuple-element.45), channel_id=1, source_target_pairs={{0,252},{1,253},{2,254},{3,255},{4,0},{5,1},{6,2},{7,3},{8,4},{9,5... | collective-permute-start | bytes 786440 | tf_op jit(solution)/shard_map/ppermute | solution.py:289
  25.3 0.0 collective-permute-done.b_ref
  25.3 0.1 add_crossed.1
  25.5 0.6 collective-permute-start.5
  26.0 2.6 %collective-permute-done.2.refs_1_ = bf16[128,1024]{1,0:T(8,128)(2,1)S(1)} collective-permute-done((bf16[128,1024]{1,0:T(8,128)(2,1)S(1)}, bf16[128,1024]{1,0:T(8,128)(2,1)S(1)}, u32[]{:S(2)}, u32[]{:S(2)}) %collective-permute-start.2) | collective-permute-done | bytes 262176 | tf_op jit(solution)/shard_map/ppermute | solution.py:279
  28.7 0.1 add_summed.1
  28.7 3.1 %collective-permute-start.3 = (bf16[128,1024]{1,0:T(8,128)(2,1)S(1)}, bf16[128,1024]{1,0:T(8,128)(2,1)S(1)}, u32[]{:S(2)}, u32[]{:S(2)}) collective-permute-start(bf16[128,1024]{1,0:T(8,128)(2,1)S(1)} %add_summed.1), channel_id=1, source_target_pairs={{0,254},{1,255},{2,252},{3,253},{4,2},{5,3},{6,0},{7,1},{8,6},{9,7... | collective-permute-start | bytes 786440 | tf_op jit(solution)/shard_map/ppermute | solution.py:289
  31.9 3.1 %early_probabilities.1 = (bf16[512,1024]{1,0:T(8,128)(2,1)S(1)}, bf16[384,1024]{1,0:T(8,128)(2,1)S(1)}, bf16[1024,128]{1,0:T(8,128)(2,1)S(1)}, bf16[1024,128]{1,...) custom-call(s32[1]{0:T(128)S(6)} %copy.10.block_ref, bf16[1,2,256,1024]{3,2,1,0:T(8,128)(2,1)} %q_hbm.3, ...), custom_call_target="tpu_custom_call" | custom-call | flops 2000000000 | bytes 1000000 | tf_op jit(solution)/shard_map/early_probabilities/pallas_call | solution.py:254
  35.0 0.0 collective-permute-done.4.do_in
  35.0 0.8 %collective-permute-done.5.do_more = bf16[128,1024]{1,0:T(8,128)(2,1)S(1)} collective-permute-done((bf16[128,1024]{1,0:T(8,128)(2,1)S(1)}, bf16[128,1024]{1,0:T(8,128)(2,1)S(1)}, u32[]{:S(2)}, u32[]{:S(2)}) %collective-permute-start.5) | collective-permute-done | bytes 262176 | tf_op jit(solution)/shard_map/ppermute | solution.py:289
  35.8 4.8 %early_bottom.1 = (bf16[128,1024]{1,0:T(8,128)(2,1)S(1)}, bf16[128,1024]{1,0:T(8,128)(2,1)S(1)}, bf16[128,1024]{1,0:T(8,128)(2,1)S(1)}, bf16[128,1024]{1,0:T(8,128)(2,1)S(1)}, f32[768,256]{1,0:T(8,128)S(1)}) custom-call(s32[1]{0:T(128)S(6)} %copy.10.block_ref, bf16[128,1024]{1,0:T(8,128)(2,1)S(1)} %collective-permute-done.4.do_in, ...), custom_call_target="tpu_custom_call" | custom-call | flops 2000000000 | bytes 1000000 | tf_op jit(solution)/shard_map/early_bottom/pallas_call | solution.py:254
  40.7 3.0 %collective-permute-start.11 = (bf16[128,1024]{1,0:T(8,128)(2,1)S(1)}, bf16[128,1024]{1,0:T(8,128)(2,1)S(1)}, u32[]{:S(2)}, u32[]{:S(2)}) collective-permute-start(bf16[128,1024]{1,0:T(8,128)(2,1)S(1)} %get-tuple-element.58), channel_id=1, source_target_pairs={{0,1},{1,0},{2,3},{3,2},{4,5},{5,4},{6,7},{7,6},{8,9},{9,8},{10,11... | collective-permute-start | bytes 786440 | tf_op jit(solution)/shard_map/ppermute | solution.py:279
  43.6 0.0 collective-permute-done.3.do_in
  43.6 4.6 %early_top.1 = (bf16[128,1024]{1,0:T(8,128)(2,1)S(1)}, bf16[128,1024]{1,0:T(8,128)(2,1)S(1)}, bf16[128,1024]{1,0:T(8,128)(2,1)S(1)}, bf16[128,1024]{1,0:T(8,128)(2,1)S(1)}, bf16[1,768,256]{2,1,0:T(8,128)(2,1)}) custom-call(s32[1]{0:T(128)S(6)} %copy.10.block_ref, bf16[128,1024]{1,0:T(8,128)(2,1)S(1)} %collective-permute-done.3.do_in, ...), custom_call_target="tpu_custom_call" | custom-call | flops 2000000000 | bytes 1000000 | tf_op jit(solution)/shard_map/early_top/pallas_call | solution.py:254
  48.2 0.0 collective-permute-start.8
  48.2 0.5 collective-permute-start.7
  48.7 0.0 collective-permute-start.6
  48.8 0.0 collective-permute-done.11
  48.8 0.1 add_convert_fusion
  48.8 1.1 %collective-permute-start.12 = (bf16[64,1024]{1,0:T(8,128)(2,1)S(1)}, bf16[64,1024]{1,0:T(8,128)(2,1)S(1)}, u32[]{:S(2)}, u32[]{:S(2)}) collective-permute-start(bf16[64,1024]{1,0:T(8,128)(2,1)S(1)} %get-tuple-element.61), channel_id=1, source_target_pairs={{0,2},{1,3},{2,0},{3,1},{4,6},{5,7},{6,4},{7,5},{8,10},{9,11},{10,... | collective-permute-start | bytes 393224 | tf_op jit(solution)/shard_map/ppermute | solution.py:279
  50.0 0.4 collective-permute-start.13
  50.4 0.0 collective-permute-done.8
  50.4 0.1 add_convert_fusion.2
  50.5 1.1 %collective-permute-start.9 = (bf16[64,1024]{1,0:T(8,128)(2,1)S(1)}, bf16[64,1024]{1,0:T(8,128)(2,1)S(1)}, u32[]{:S(2)}, u32[]{:S(2)}) collective-permute-start(bf16[64,1024]{1,0:T(8,128)(2,1)S(1)} %get-tuple-element.63), channel_id=1, source_target_pairs={{0,2},{1,3},{2,0},{3,1},{4,6},{5,7},{6,4},{7,5},{8,10},{9,11},{10,... | collective-permute-start | bytes 393224 | tf_op jit(solution)/shard_map/ppermute | solution.py:279
  51.6 0.0 collective-permute-done.7.got_b
  51.6 0.4 collective-permute-start.10
  52.0 1.5 %collective-permute-done.12.refs_2_ = bf16[64,1024]{1,0:T(8,128)(2,1)S(1)} collective-permute-done((bf16[64,1024]{1,0:T(8,128)(2,1)S(1)}, bf16[64,1024]{1,0:T(8,128)(2,1)S(1)}, u32[]{:S(2)}, u32[]{:S(2)}) %collective-permute-start.12) | collective-permute-done | bytes 131104 | tf_op jit(solution)/shard_map/ppermute | solution.py:279
  53.5 2.8 %collective-permute-done.13.refs_3_ = bf16[64,1024]{1,0:T(8,128)(2,1)S(1)} collective-permute-done((bf16[64,1024]{1,0:T(8,128)(2,1)S(1)}, bf16[64,1024]{1,0:T(8,128)(2,1)S(1)}, u32[]{:S(2)}, u32[]{:S(2)}) %collective-permute-start.13) | collective-permute-done | bytes 131104 | tf_op jit(solution)/shard_map/ppermute | solution.py:279
  56.3 0.0 collective-permute-done.6.got_t
  56.3 2.8 %collective-permute-done.9.refs_0_ = bf16[64,1024]{1,0:T(8,128)(2,1)S(1)} collective-permute-done((bf16[64,1024]{1,0:T(8,128)(2,1)S(1)}, bf16[64,1024]{1,0:T(8,128)(2,1)S(1)}, u32[]{:S(2)}, u32[]{:S(2)}) %collective-permute-start.9) | collective-permute-done | bytes 131104 | tf_op jit(solution)/shard_map/ppermute | solution.py:279
  59.1 2.8 %collective-permute-done.10.refs_1_ = bf16[64,1024]{1,0:T(8,128)(2,1)S(1)} collective-permute-done((bf16[64,1024]{1,0:T(8,128)(2,1)S(1)}, bf16[64,1024]{1,0:T(8,128)(2,1)S(1)}, u32[]{:S(2)}, u32[]{:S(2)}) %collective-permute-start.10) | collective-permute-done | bytes 131104 | tf_op jit(solution)/shard_map/ppermute | solution.py:279
  61.9 1.0 %finish.1 = bf16[1,256,1024]{2,1,0:T(8,128)(2,1)} custom-call(bf16[128,1024]{1,0:T(8,128)(2,1)S(1)} %get-tuple-element.51.keep_t, bf16[128,1024]{1,0:T(8,128)(2,1)S(1)} %collective-permute-done.6.got_t, bf16[128,1024]{1,0:T(8,128)(2,1)S(1)} %get-tuple-element.53.keep_b, bf16[128,1024]{1,0:T(8,128)(2,1)S(1)} %collective-permute-done.7.got_b, ...), custom_call_target="tpu_custom_call" | custom-call | flops 2000000000 | bytes 1000000 | tf_op jit(solution)/shard_map/finish/pallas_call | solution.py:254
Async XLA Ops:
  10.5 5.0 %collective-permute-start.1 = (bf16[256,1024]{1,0:T(8,128)(2,1)S(1)}, bf16[256,1024]{1,0:T(8,128)(2,1)S(1)}, u32[]{:S(2)}, u32[]{:S(2)}) collective-permute-start(bf16[256,1024]{1,0:T(8,128)(2,1)S(1)} %get-tuple-element.39), channel_id=1, source_target_pairs={{0,1},{1,0},{2,3},{3,2},{4,5},{5,4},{6,7},{7,6},{8,9},{9,8},{10,11... | collective-permute-start | bytes 1572872 | tf_op jit(solution)/shard_map/ppermute | solution.py:279
  15.3 10.0 %collective-permute-start = (bf16[256,1024]{1,0:T(8,128)(2,1)S(1)}, bf16[256,1024]{1,0:T(8,128)(2,1)S(1)}, u32[]{:S(2)}, u32[]{:S(2)}) collective-permute-start(bf16[256,1024]{1,0:T(8,128)(2,1)S(1)} %get-tuple-element.36), channel_id=1, source_target_pairs={{0,1},{1,0},{2,3},{3,2},{4,5},{5,4},{6,7},{7,6},{8,9},{9,8},{10,11... | collective-permute-start | bytes 1572872 | tf_op jit(solution)/shard_map/ppermute | solution.py:279
  15.6 13.1 %collective-permute-start.2 = (bf16[128,1024]{1,0:T(8,128)(2,1)S(1)}, bf16[128,1024]{1,0:T(8,128)(2,1)S(1)}, u32[]{:S(2)}, u32[]{:S(2)}) collective-permute-start(bf16[128,1024]{1,0:T(8,128)(2,1)S(1)} %get-tuple-element.40), channel_id=1, source_target_pairs={{0,2},{1,3},{2,0},{3,1},{4,6},{5,7},{6,4},{7,5},{8,10},{9,11},{10,... | collective-permute-start | bytes 786440 | tf_op jit(solution)/shard_map/ppermute | solution.py:279
  15.7 19.3 %collective-permute-start.4 = (bf16[128,1024]{1,0:T(8,128)(2,1)S(1)}, bf16[128,1024]{1,0:T(8,128)(2,1)S(1)}, u32[]{:S(2)}, u32[]{:S(2)}) collective-permute-start(bf16[128,1024]{1,0:T(8,128)(2,1)S(1)} %get-tuple-element.45), channel_id=1, source_target_pairs={{0,252},{1,253},{2,254},{3,255},{4,0},{5,1},{6,2},{7,3},{8,4},{9,5... | collective-permute-start | bytes 786440 | tf_op jit(solution)/shard_map/ppermute | solution.py:289
  25.5 10.4 %collective-permute-start.5 = (bf16[128,1024]{1,0:T(8,128)(2,1)S(1)}, bf16[128,1024]{1,0:T(8,128)(2,1)S(1)}, u32[]{:S(2)}, u32[]{:S(2)}) collective-permute-start(bf16[128,1024]{1,0:T(8,128)(2,1)S(1)} %get-tuple-element.46), channel_id=1, source_target_pairs={{0,254},{1,255},{2,252},{3,253},{4,2},{5,3},{6,0},{7,1},{8,6},{9,7... | collective-permute-start | bytes 786440 | tf_op jit(solution)/shard_map/ppermute | solution.py:289
  28.7 14.9 %collective-permute-start.3 = (bf16[128,1024]{1,0:T(8,128)(2,1)S(1)}, bf16[128,1024]{1,0:T(8,128)(2,1)S(1)}, u32[]{:S(2)}, u32[]{:S(2)}) collective-permute-start(bf16[128,1024]{1,0:T(8,128)(2,1)S(1)} %add_summed.1), channel_id=1, source_target_pairs={{0,254},{1,255},{2,252},{3,253},{4,2},{5,3},{6,0},{7,1},{8,6},{9,7... | collective-permute-start | bytes 786440 | tf_op jit(solution)/shard_map/ppermute | solution.py:289
  40.7 8.1 %collective-permute-start.11 = (bf16[128,1024]{1,0:T(8,128)(2,1)S(1)}, bf16[128,1024]{1,0:T(8,128)(2,1)S(1)}, u32[]{:S(2)}, u32[]{:S(2)}) collective-permute-start(bf16[128,1024]{1,0:T(8,128)(2,1)S(1)} %get-tuple-element.58), channel_id=1, source_target_pairs={{0,1},{1,0},{2,3},{3,2},{4,5},{5,4},{6,7},{7,6},{8,9},{9,8},{10,11... | collective-permute-start | bytes 786440 | tf_op jit(solution)/shard_map/ppermute | solution.py:279
  48.2 2.2 %collective-permute-start.8 = (bf16[128,1024]{1,0:T(8,128)(2,1)S(1)}, bf16[128,1024]{1,0:T(8,128)(2,1)S(1)}, u32[]{:S(2)}, u32[]{:S(2)}) collective-permute-start(bf16[128,1024]{1,0:T(8,128)(2,1)S(1)} %get-tuple-element.56), channel_id=1, source_target_pairs={{0,1},{1,0},{2,3},{3,2},{4,5},{5,4},{6,7},{7,6},{8,9},{9,8},{10,11... | collective-permute-start | bytes 786440 | tf_op jit(solution)/shard_map/ppermute | solution.py:279
  48.2 3.4 %collective-permute-start.7 = (bf16[128,1024]{1,0:T(8,128)(2,1)S(1)}, bf16[128,1024]{1,0:T(8,128)(2,1)S(1)}, u32[]{:S(2)}, u32[]{:S(2)}) collective-permute-start(bf16[128,1024]{1,0:T(8,128)(2,1)S(1)} %get-tuple-element.54), channel_id=1, source_target_pairs={{0,1},{1,0},{2,3},{3,2},{4,5},{5,4},{6,7},{7,6},{8,9},{9,8},{10,11... | collective-permute-start | bytes 786440 | tf_op jit(solution)/shard_map/ppermute | solution.py:279
  48.7 7.6 %collective-permute-start.6 = (bf16[128,1024]{1,0:T(8,128)(2,1)S(1)}, bf16[128,1024]{1,0:T(8,128)(2,1)S(1)}, u32[]{:S(2)}, u32[]{:S(2)}) collective-permute-start(bf16[128,1024]{1,0:T(8,128)(2,1)S(1)} %get-tuple-element.52), channel_id=1, source_target_pairs={{0,1},{1,0},{2,3},{3,2},{4,5},{5,4},{6,7},{7,6},{8,9},{9,8},{10,11... | collective-permute-start | bytes 786440 | tf_op jit(solution)/shard_map/ppermute | solution.py:279
  48.8 4.7 %collective-permute-start.12 = (bf16[64,1024]{1,0:T(8,128)(2,1)S(1)}, bf16[64,1024]{1,0:T(8,128)(2,1)S(1)}, u32[]{:S(2)}, u32[]{:S(2)}) collective-permute-start(bf16[64,1024]{1,0:T(8,128)(2,1)S(1)} %get-tuple-element.61), channel_id=1, source_target_pairs={{0,2},{1,3},{2,0},{3,1},{4,6},{5,7},{6,4},{7,5},{8,10},{9,11},{10,... | collective-permute-start | bytes 393224 | tf_op jit(solution)/shard_map/ppermute | solution.py:279
  50.0 6.3 %collective-permute-start.13 = (bf16[64,1024]{1,0:T(8,128)(2,1)S(1)}, bf16[64,1024]{1,0:T(8,128)(2,1)S(1)}, u32[]{:S(2)}, u32[]{:S(2)}) collective-permute-start(bf16[64,1024]{1,0:T(8,128)(2,1)S(1)} %get-tuple-element.60), channel_id=1, source_target_pairs={{0,2},{1,3},{2,0},{3,1},{4,6},{5,7},{6,4},{7,5},{8,10},{9,11},{10,... | collective-permute-start | bytes 393224 | tf_op jit(solution)/shard_map/ppermute | solution.py:279
  50.5 8.6 %collective-permute-start.9 = (bf16[64,1024]{1,0:T(8,128)(2,1)S(1)}, bf16[64,1024]{1,0:T(8,128)(2,1)S(1)}, u32[]{:S(2)}, u32[]{:S(2)}) collective-permute-start(bf16[64,1024]{1,0:T(8,128)(2,1)S(1)} %get-tuple-element.63), channel_id=1, source_target_pairs={{0,2},{1,3},{2,0},{3,1},{4,6},{5,7},{6,4},{7,5},{8,10},{9,11},{10,... | collective-permute-start | bytes 393224 | tf_op jit(solution)/shard_map/ppermute | solution.py:279
  51.6 10.3 %collective-permute-start.10 = (bf16[64,1024]{1,0:T(8,128)(2,1)S(1)}, bf16[64,1024]{1,0:T(8,128)(2,1)S(1)}, u32[]{:S(2)}, u32[]{:S(2)}) collective-permute-start(bf16[64,1024]{1,0:T(8,128)(2,1)S(1)} %get-tuple-element.62), channel_id=1, source_target_pairs={{0,2},{1,3},{2,0},{3,1},{4,6},{5,7},{6,4},{7,5},{8,10},{9,11},{10,... | collective-permute-start | bytes 393224 | tf_op jit(solution)/shard_map/ppermute | solution.py:279

commit v4 on v3

--- a/solution.py
+++ b/solution.py
@@ -13,7 +13,7 @@
 WIDTH = 1024
 KV_WIDTH = 256
 HALVES = ((128, 256), (0, 128))
-PIECES = 4
+PIECES = 2
 NT = (((1,), (1,)), ((), ()))
 NN = (((1,), (0,)), ((), ()))
 
@@ -344,7 +344,6 @@
         add_halves, "add_crossed", [VMEM] * 2, [keep2, got2], [half_block, half_block], [], 4
     )
     crossed = shift_down(crossed, 2)
-    summed = shift_down(add("add_summed", kept, other), 2)
     p_b, p_t, q_b, q_t, kv_held, top_held = call(
         early_probabilities,
         "early_probabilities",
@@ -354,6 +353,8 @@
         [pltpu.SemaphoreType.DMA((2,)), pltpu.SemaphoreType.DMA((2, WIDTH // HD))],
         10,
     )
+    kept, p_t = lax.optimization_barrier((kept, p_t))
+    summed = shift_down(add("add_summed", kept, other), 2)
     half_scratch = [
         pltpu.VMEM(*half_block),
         pltpu.VMEM(*half_block),

time: 63 us -> 63 us (level)
  starting transfers between devices: 23.5 us -> 22.2 us
  waiting for transfers between devices: 13.4 us -> 14.6 us
    ppermute x3, waiting for transfers between devices: 0.8 us -> 3.67 us  [shift_down(): return lax.ppermute(block, ('section', 'tp'), route)]
    ppermute x11 -> x9, waiting for transfers between devices: 12.6 us -> 11 us  [swap(): lax.ppermute(block, 'tp', [(i, i ^ mask) for i in range(lax.axis_size('tp...]
    ppermute x11 -> x9, starting transfers between devices: 10.2 us -> 9.1 us  [swap(): lax.ppermute(block, 'tp', [(i, i ^ mask) for i in range(lax.axis_size('tp...]
  transfers between devices with their start and end apart: 14 -> 12, of which waited for: 6 -> 3; matrix products, arithmetic and copies ran while one was open for 0% -> 0% of each run, Pallas kernels for 23% -> 23%
where the time goes in v4:
time: 63 us; the launch traced here: 62.9 us
  Pallas kernels  24.6 us (39%)
  starting transfers between devices  22.2 us (35%)
  waiting for transfers between devices  14.6 us (23%)
  between operations  1.37 us (2%)
    pallas_call x9, Pallas kernels, call(): pl.pallas_call(kernel, out_shape=[pltpu.HBM(*out[:2]) if len(out) > 2 els...  24.6 us
    ppermute x3, starting transfers between devices, shift_down(): return lax.ppermute(block, ('section', 'tp'), route)  13.1 us
    ppermute x9, waiting for transfers between devices, swap(): lax.ppermute(block, 'tp', [(i, i ^ mask) for i in range(lax.axis_size('tp...  11 us
    ppermute x9, starting transfers between devices, swap(): lax.ppermute(block, 'tp', [(i, i ^ mask) for i in range(lax.axis_size('tp...  9.1 us
    ppermute x3, waiting for transfers between devices, shift_down(): return lax.ppermute(block, ('section', 'tp'), route)  3.67 us
  transfers between devices with their start and end apart: 12, of which 3 were waited for; matrix products, arithmetic and copies ran while one was open for 0% of the time, Pallas kernels for 23%

profile of v4, /device:TPU:1, one launch (start us, length us, event | category | flops | bytes accessed | tf_op | source)
XLA Modules:
  0.0 62.9 jit_solution(6231517970818856475)
XLA Ops:
  1.3 9.2 %late_first.1 = (bf16[256,1024]{1,0:T(8,128)(2,1)S(1)}, bf16[256,1024]{1,0:T(8,128)(2,1)S(1)}, f32[768,256]{1,0:T(8,128)S(1)}, bf16[256,1024]{1,0:T(8,128)(2,1)S...) custom-call(s32[1]{0:T(128)S(6)} %copy.10.block_ref, ...), custom_call_target="tpu_custom_call" | custom-call | flops 2000000000 | bytes 1000000 | tf_op jit(solution)/shard_map/late_first/pallas_call | solution.py:254
  10.5 3.3 %collective-permute-start.1 = (bf16[256,1024]{1,0:T(8,128)(2,1)S(1)}, bf16[256,1024]{1,0:T(8,128)(2,1)S(1)}, u32[]{:S(2)}, u32[]{:S(2)}) collective-permute-start(bf16[256,1024]{1,0:T(8,128)(2,1)S(1)} %get-tuple-element.43), channel_id=1, source_target_pairs={{0,1},{1,0},{2,3},{3,2},{4,5},{5,4},{6,7},{7,6},{8,9},{9,8},{10,11... | collective-permute-start | bytes 1572872 | tf_op jit(solution)/shard_map/ppermute | solution.py:279
  13.8 1.5 %late_second.1 = (bf16[256,1024]{1,0:T(8,128)(2,1)S(1)}, bf16[256,1024]{1,0:T(8,128)(2,1)S(1)}) custom-call(bf16[256,1024]{1,0:T(8,128)(2,1)S(1)} %get-tuple-element.33.dq_ref, bf16[256,256]{1,0:T(8,128)(2,1)S(1)} %get-tuple-element.34.own_ref, bf16[4,1024,1024]{2,1,0:T(8,128)(2,1)S(1)} %get-tuple-element.35.wq, bf16[4,1024,256]{2,1,0:T(8,128)(2,1)S(1)} %get-tuple-element.36.wkv), custom_call_target="tpu_custom_call" | custom-call | flops 2000000000 | bytes 1000000 | tf_op jit(solution)/shard_map/late_second/pallas_call | solution.py:254
  15.3 0.1 collective-permute-start
  15.4 0.0 collective-permute-done.1.b_ref
  15.5 0.1 add_mine.1
  15.6 0.1 collective-permute-start.2
  15.7 9.7 %collective-permute-start.4 = (bf16[128,1024]{1,0:T(8,128)(2,1)S(1)}, bf16[128,1024]{1,0:T(8,128)(2,1)S(1)}, u32[]{:S(2)}, u32[]{:S(2)}) collective-permute-start(bf16[128,1024]{1,0:T(8,128)(2,1)S(1)} %get-tuple-element.49), channel_id=1, source_target_pairs={{0,252},{1,253},{2,254},{3,255},{4,0},{5,1},{6,2},{7,3},{8,4},{9,5... | collective-permute-start | bytes 786440 | tf_op jit(solution)/shard_map/ppermute | solution.py:289
  25.3 0.0 collective-permute-done.b_ref
  25.3 0.1 add_crossed.1
  25.5 0.7 %collective-permute-start.5 = (bf16[128,1024]{1,0:T(8,128)(2,1)S(1)}, bf16[128,1024]{1,0:T(8,128)(2,1)S(1)}, u32[]{:S(2)}, u32[]{:S(2)}) collective-permute-start(bf16[128,1024]{1,0:T(8,128)(2,1)S(1)} %get-tuple-element.50), channel_id=1, source_target_pairs={{0,254},{1,255},{2,252},{3,253},{4,2},{5,3},{6,0},{7,1},{8,6},{9,7... | collective-permute-start | bytes 786440 | tf_op jit(solution)/shard_map/ppermute | solution.py:289
  26.2 3.1 %early_probabilities.1 = (bf16[512,1024]{1,0:T(8,128)(2,1)S(1)}, bf16[384,1024]{1,0:T(8,128)(2,1)S(1)}, bf16[1024,128]{1,0:T(8,128)(2,1)S(1)}, bf16[1024,128]{1,...) custom-call(s32[1]{0:T(128)S(6)} %copy.10.block_ref, bf16[1,2,256,1024]{3,2,1,0:T(8,128)(2,1)} %q_hbm.3, ...), custom_call_target="tpu_custom_call" | custom-call | flops 2000000000 | bytes 1000000 | tf_op jit(solution)/shard_map/early_probabilities/pallas_call | solution.py:254
  29.4 0.0 collective-permute-done.2.refs_1_
  29.4 0.1 add_summed.1
  29.4 2.7 %collective-permute-start.3 = (bf16[128,1024]{1,0:T(8,128)(2,1)S(1)}, bf16[128,1024]{1,0:T(8,128)(2,1)S(1)}, u32[]{:S(2)}, u32[]{:S(2)}) collective-permute-start(bf16[128,1024]{1,0:T(8,128)(2,1)S(1)} %add_summed.1), channel_id=1, source_target_pairs={{0,254},{1,255},{2,252},{3,253},{4,2},{5,3},{6,0},{7,1},{8,6},{9,7... | collective-permute-start | bytes 786440 | tf_op jit(solution)/shard_map/ppermute | solution.py:289
  32.2 0.0 collective-permute-done.4.do_in
  32.2 3.7 %collective-permute-done.5.do_more = bf16[128,1024]{1,0:T(8,128)(2,1)S(1)} collective-permute-done((bf16[128,1024]{1,0:T(8,128)(2,1)S(1)}, bf16[128,1024]{1,0:T(8,128)(2,1)S(1)}, u32[]{:S(2)}, u32[]{:S(2)}) %collective-permute-start.5) | collective-permute-done | bytes 262176 | tf_op jit(solution)/shard_map/ppermute | solution.py:289
  35.8 4.8 %early_bottom.1 = (bf16[128,1024]{1,0:T(8,128)(2,1)S(1)}, bf16[128,1024]{1,0:T(8,128)(2,1)S(1)}, bf16[128,1024]{1,0:T(8,128)(2,1)S(1)}, bf16[128,1024]{1,0:T(8,128)(2,1)S(1)}, f32[768,256]{1,0:T(8,128)S(1)}) custom-call(s32[1]{0:T(128)S(6)} %copy.10.block_ref, bf16[128,1024]{1,0:T(8,128)(2,1)S(1)} %collective-permute-done.4.do_in, ...), custom_call_target="tpu_custom_call" | custom-call | flops 2000000000 | bytes 1000000 | tf_op jit(solution)/shard_map/early_bottom/pallas_call | solution.py:254
  40.7 3.0 %collective-permute-start.10 = (bf16[128,1024]{1,0:T(8,128)(2,1)S(1)}, bf16[128,1024]{1,0:T(8,128)(2,1)S(1)}, u32[]{:S(2)}, u32[]{:S(2)}) collective-permute-start(bf16[128,1024]{1,0:T(8,128)(2,1)S(1)} %get-tuple-element.62), channel_id=1, source_target_pairs={{0,1},{1,0},{2,3},{3,2},{4,5},{5,4},{6,7},{7,6},{8,9},{9,8},{10,11... | collective-permute-start | bytes 786440 | tf_op jit(solution)/shard_map/ppermute | solution.py:279
  43.6 0.0 collective-permute-done.3.do_in
  43.6 4.6 %early_top.1 = (bf16[128,1024]{1,0:T(8,128)(2,1)S(1)}, bf16[128,1024]{1,0:T(8,128)(2,1)S(1)}, bf16[128,1024]{1,0:T(8,128)(2,1)S(1)}, bf16[128,1024]{1,0:T(8,128)(2,1)S(1)}, bf16[1,768,256]{2,1,0:T(8,128)(2,1)}) custom-call(s32[1]{0:T(128)S(6)} %copy.10.block_ref, bf16[128,1024]{1,0:T(8,128)(2,1)S(1)} %collective-permute-done.3.do_in, ...), custom_call_target="tpu_custom_call" | custom-call | flops 2000000000 | bytes 1000000 | tf_op jit(solution)/shard_map/early_top/pallas_call | solution.py:254
  48.2 0.0 collective-permute-start.8
  48.2 0.5 collective-permute-start.7
  48.7 0.0 collective-permute-start.6
  48.8 0.0 collective-permute-done.10
  48.8 0.1 add_convert_fusion
  48.8 1.1 %collective-permute-start.11 = (bf16[128,1024]{1,0:T(8,128)(2,1)S(1)}, bf16[128,1024]{1,0:T(8,128)(2,1)S(1)}, u32[]{:S(2)}, u32[]{:S(2)}) collective-permute-start(bf16[128,1024]{1,0:T(8,128)(2,1)S(1)} %add_convert_fusion), channel_id=1, source_target_pairs={{0,2},{1,3},{2,0},{3,1},{4,6},{5,7},{6,4},{7,5},{8,10},{9,11},{10,... | collective-permute-start | bytes 786440 | tf_op jit(solution)/shard_map/ppermute | solution.py:279
  50.0 0.0 collective-permute-done.8
  50.0 0.1 add_convert_fusion.1
  50.0 0.9 %collective-permute-start.9 = (bf16[128,1024]{1,0:T(8,128)(2,1)S(1)}, bf16[128,1024]{1,0:T(8,128)(2,1)S(1)}, u32[]{:S(2)}, u32[]{:S(2)}) collective-permute-start(bf16[128,1024]{1,0:T(8,128)(2,1)S(1)} %add_convert_fusion.1), channel_id=1, source_target_pairs={{0,2},{1,3},{2,0},{3,1},{4,6},{5,7},{6,4},{7,5},{8,10},{9,11},{10,... | collective-permute-start | bytes 786440 | tf_op jit(solution)/shard_map/ppermute | solution.py:279
  51.0 0.0 collective-permute-done.7.got_b
  51.0 0.0 collective-permute-done.6.got_t
  51.0 5.3 %collective-permute-done.11.refs_1_ = bf16[128,1024]{1,0:T(8,128)(2,1)S(1)} collective-permute-done((bf16[128,1024]{1,0:T(8,128)(2,1)S(1)}, bf16[128,1024]{1,0:T(8,128)(2,1)S(1)}, u32[]{:S(2)}, u32[]{:S(2)}) %collective-permute-start.11) | collective-permute-done | bytes 262176 | tf_op jit(solution)/shard_map/ppermute | solution.py:279
  56.3 5.6 %collective-permute-done.9.refs_0_ = bf16[128,1024]{1,0:T(8,128)(2,1)S(1)} collective-permute-done((bf16[128,1024]{1,0:T(8,128)(2,1)S(1)}, bf16[128,1024]{1,0:T(8,128)(2,1)S(1)}, u32[]{:S(2)}, u32[]{:S(2)}) %collective-permute-start.9) | collective-permute-done | bytes 262176 | tf_op jit(solution)/shard_map/ppermute | solution.py:279
  61.9 1.0 %finish.1 = bf16[1,256,1024]{2,1,0:T(8,128)(2,1)} custom-call(bf16[128,1024]{1,0:T(8,128)(2,1)S(1)} %get-tuple-element.55.keep_t, bf16[128,1024]{1,0:T(8,128)(2,1)S(1)} %collective-permute-done.6.got_t, bf16[128,1024]{1,0:T(8,128)(2,1)S(1)} %get-tuple-element.57.keep_b, bf16[128,1024]{1,0:T(8,128)(2,1)S(1)} %collective-permute-done.7.got_b, ...), custom_call_target="tpu_custom_call" | custom-call | flops 2000000000 | bytes 1000000 | tf_op jit(solution)/shard_map/finish/pallas_call | solution.py:254
Async XLA Ops:
  10.5 5.0 %collective-permute-start.1 = (bf16[256,1024]{1,0:T(8,128)(2,1)S(1)}, bf16[256,1024]{1,0:T(8,128)(2,1)S(1)}, u32[]{:S(2)}, u32[]{:S(2)}) collective-permute-start(bf16[256,1024]{1,0:T(8,128)(2,1)S(1)} %get-tuple-element.43), channel_id=1, source_target_pairs={{0,1},{1,0},{2,3},{3,2},{4,5},{5,4},{6,7},{7,6},{8,9},{9,8},{10,11... | collective-permute-start | bytes 1572872 | tf_op jit(solution)/shard_map/ppermute | solution.py:279
  15.3 10.0 %collective-permute-start = (bf16[256,1024]{1,0:T(8,128)(2,1)S(1)}, bf16[256,1024]{1,0:T(8,128)(2,1)S(1)}, u32[]{:S(2)}, u32[]{:S(2)}) collective-permute-start(bf16[256,1024]{1,0:T(8,128)(2,1)S(1)} %get-tuple-element.38), channel_id=1, source_target_pairs={{0,1},{1,0},{2,3},{3,2},{4,5},{5,4},{6,7},{7,6},{8,9},{9,8},{10,11... | collective-permute-start | bytes 1572872 | tf_op jit(solution)/shard_map/ppermute | solution.py:279
  15.6 13.8 %collective-permute-start.2 = (bf16[128,1024]{1,0:T(8,128)(2,1)S(1)}, bf16[128,1024]{1,0:T(8,128)(2,1)S(1)}, u32[]{:S(2)}, u32[]{:S(2)}) collective-permute-start(bf16[128,1024]{1,0:T(8,128)(2,1)S(1)} %get-tuple-element.44), channel_id=1, source_target_pairs={{0,2},{1,3},{2,0},{3,1},{4,6},{5,7},{6,4},{7,5},{8,10},{9,11},{10,... | collective-permute-start | bytes 786440 | tf_op jit(solution)/shard_map/ppermute | solution.py:279
  15.7 16.5 %collective-permute-start.4 = (bf16[128,1024]{1,0:T(8,128)(2,1)S(1)}, bf16[128,1024]{1,0:T(8,128)(2,1)S(1)}, u32[]{:S(2)}, u32[]{:S(2)}) collective-permute-start(bf16[128,1024]{1,0:T(8,128)(2,1)S(1)} %get-tuple-element.49), channel_id=1, source_target_pairs={{0,252},{1,253},{2,254},{3,255},{4,0},{5,1},{6,2},{7,3},{8,4},{9,5... | collective-permute-start | bytes 786440 | tf_op jit(solution)/shard_map/ppermute | solution.py:289
  25.5 10.4 %collective-permute-start.5 = (bf16[128,1024]{1,0:T(8,128)(2,1)S(1)}, bf16[128,1024]{1,0:T(8,128)(2,1)S(1)}, u32[]{:S(2)}, u32[]{:S(2)}) collective-permute-start(bf16[128,1024]{1,0:T(8,128)(2,1)S(1)} %get-tuple-element.50), channel_id=1, source_target_pairs={{0,254},{1,255},{2,252},{3,253},{4,2},{5,3},{6,0},{7,1},{8,6},{9,7... | collective-permute-start | bytes 786440 | tf_op jit(solution)/shard_map/ppermute | solution.py:289
  29.4 14.2 %collective-permute-start.3 = (bf16[128,1024]{1,0:T(8,128)(2,1)S(1)}, bf16[128,1024]{1,0:T(8,128)(2,1)S(1)}, u32[]{:S(2)}, u32[]{:S(2)}) collective-permute-start(bf16[128,1024]{1,0:T(8,128)(2,1)S(1)} %add_summed.1), channel_id=1, source_target_pairs={{0,254},{1,255},{2,252},{3,253},{4,2},{5,3},{6,0},{7,1},{8,6},{9,7... | collective-permute-start | bytes 786440 | tf_op jit(solution)/shard_map/ppermute | solution.py:289
  40.7 8.1 %collective-permute-start.10 = (bf16[128,1024]{1,0:T(8,128)(2,1)S(1)}, bf16[128,1024]{1,0:T(8,128)(2,1)S(1)}, u32[]{:S(2)}, u32[]{:S(2)}) collective-permute-start(bf16[128,1024]{1,0:T(8,128)(2,1)S(1)} %get-tuple-element.62), channel_id=1, source_target_pairs={{0,1},{1,0},{2,3},{3,2},{4,5},{5,4},{6,7},{7,6},{8,9},{9,8},{10,11... | collective-permute-start | bytes 786440 | tf_op jit(solution)/shard_map/ppermute | solution.py:279
  48.2 1.8 %collective-permute-start.8 = (bf16[128,1024]{1,0:T(8,128)(2,1)S(1)}, bf16[128,1024]{1,0:T(8,128)(2,1)S(1)}, u32[]{:S(2)}, u32[]{:S(2)}) collective-permute-start(bf16[128,1024]{1,0:T(8,128)(2,1)S(1)} %get-tuple-element.60), channel_id=1, source_target_pairs={{0,1},{1,0},{2,3},{3,2},{4,5},{5,4},{6,7},{7,6},{8,9},{9,8},{10,11... | collective-permute-start | bytes 786440 | tf_op jit(solution)/shard_map/ppermute | solution.py:279
  48.2 2.7 %collective-permute-start.7 = (bf16[128,1024]{1,0:T(8,128)(2,1)S(1)}, bf16[128,1024]{1,0:T(8,128)(2,1)S(1)}, u32[]{:S(2)}, u32[]{:S(2)}) collective-permute-start(bf16[128,1024]{1,0:T(8,128)(2,1)S(1)} %get-tuple-element.58), channel_id=1, source_target_pairs={{0,1},{1,0},{2,3},{3,2},{4,5},{5,4},{6,7},{7,6},{8,9},{9,8},{10,11... | collective-permute-start | bytes 786440 | tf_op jit(solution)/shard_map/ppermute | solution.py:279
  48.7 2.2 %collective-permute-start.6 = (bf16[128,1024]{1,0:T(8,128)(2,1)S(1)}, bf16[128,1024]{1,0:T(8,128)(2,1)S(1)}, u32[]{:S(2)}, u32[]{:S(2)}) collective-permute-start(bf16[128,1024]{1,0:T(8,128)(2,1)S(1)} %get-tuple-element.56), channel_id=1, source_target_pairs={{0,1},{1,0},{2,3},{3,2},{4,5},{5,4},{6,7},{7,6},{8,9},{9,8},{10,11... | collective-permute-start | bytes 786440 | tf_op jit(solution)/shard_map/ppermute | solution.py:279
  48.8 7.5 %collective-permute-start.11 = (bf16[128,1024]{1,0:T(8,128)(2,1)S(1)}, bf16[128,1024]{1,0:T(8,128)(2,1)S(1)}, u32[]{:S(2)}, u32[]{:S(2)}) collective-permute-start(bf16[128,1024]{1,0:T(8,128)(2,1)S(1)} %add_convert_fusion), channel_id=1, source_target_pairs={{0,2},{1,3},{2,0},{3,1},{4,6},{5,7},{6,4},{7,5},{8,10},{9,11},{10,... | collective-permute-start | bytes 786440 | tf_op jit(solution)/shard_map/ppermute | solution.py:279
  50.0 11.9 %collective-permute-start.9 = (bf16[128,1024]{1,0:T(8,128)(2,1)S(1)}, bf16[128,1024]{1,0:T(8,128)(2,1)S(1)}, u32[]{:S(2)}, u32[]{:S(2)}) collective-permute-start(bf16[128,1024]{1,0:T(8,128)(2,1)S(1)} %add_convert_fusion.1), channel_id=1, source_target_pairs={{0,2},{1,3},{2,0},{3,1},{4,6},{5,7},{6,4},{7,5},{8,10},{9,11},{10,... | collective-permute-start | bytes 786440 | tf_op jit(solution)/shard_map/ppermute | solution.py:279

commit v5 on v4

--- a/solution.py
+++ b/solution.py
@@ -31,7 +31,9 @@
 
 def probabilities(key_rows, q_g, bias):
     scale = math.log2(math.e) / math.sqrt(HD)
-    s = dot(key_rows, q_g, NT) * scale + bias
+    s = dot(key_rows, q_g, NT) * scale
+    always = s.shape[0] - bias.shape[0]
+    s = s + bias if always == 0 else jnp.concatenate([s[:always], s[always:] + bias], axis=0)
     e = jnp.exp2(s - jnp.max(s, axis=0, keepdims=True))
     return e * (1.0 / jnp.sum(e, axis=0, keepdims=True))
 
@@ -114,7 +116,7 @@
     carry_copy.start()
     first_row = (block_ref[0] + 1) * BLOCK
     keys = 3 * BLOCK
-    bias = visible_bias(keys, first_row, BLOCK, BLOCK)
+    bias = visible_bias(keys - BLOCK, first_row - BLOCK, BLOCK, BLOCK)
     kv_copy.wait()
     wait_all(copies)
     start_all(loads)

time: 63 us -> 63.1 us (level)
  no operation moved by 1% of the time
where the time goes in v5:
time: 63.1 us; the launch traced here: 62.9 us
  Pallas kernels  24.6 us (39%)
  starting transfers between devices  22.2 us (35%)
  waiting for transfers between devices  14.6 us (23%)
  between operations  1.37 us (2%)
    pallas_call x9, Pallas kernels, call(): pl.pallas_call(kernel, out_shape=[pltpu.HBM(*out[:2]) if len(out) > 2 els...  24.6 us
    ppermute x3, starting transfers between devices, shift_down(): return lax.ppermute(block, ('section', 'tp'), route)  13.1 us
    ppermute x9, waiting for transfers between devices, swap(): lax.ppermute(block, 'tp', [(i, i ^ mask) for i in range(lax.axis_size('tp...  11 us
    ppermute x9, starting transfers between devices, swap(): lax.ppermute(block, 'tp', [(i, i ^ mask) for i in range(lax.axis_size('tp...  9.1 us
    ppermute x3, waiting for transfers between devices, shift_down(): return lax.ppermute(block, ('section', 'tp'), route)  3.67 us
  transfers between devices with their start and end apart: 12, of which 3 were waited for; matrix products, arithmetic and copies ran while one was open for 0% of the time, Pallas kernels for 23%

profile of v5, /device:TPU:1, one launch (start us, length us, event | category | flops | bytes accessed | tf_op | source)
XLA Modules:
  0.0 62.9 jit_solution(14536697582671582974)
XLA Ops:
  1.3 9.2 %late_first.1 = (bf16[256,1024]{1,0:T(8,128)(2,1)S(1)}, bf16[256,1024]{1,0:T(8,128)(2,1)S(1)}, f32[768,256]{1,0:T(8,128)S(1)}, bf16[256,1024]{1,0:T(8,128)(2,1)S...) custom-call(s32[1]{0:T(128)S(6)} %copy.10.block_ref, ...), custom_call_target="tpu_custom_call" | custom-call | flops 2000000000 | bytes 1000000 | tf_op jit(solution)/shard_map/late_first/pallas_call | solution.py:256
  10.5 3.3 %collective-permute-start.1 = (bf16[256,1024]{1,0:T(8,128)(2,1)S(1)}, bf16[256,1024]{1,0:T(8,128)(2,1)S(1)}, u32[]{:S(2)}, u32[]{:S(2)}) collective-permute-start(bf16[256,1024]{1,0:T(8,128)(2,1)S(1)} %get-tuple-element.43), channel_id=1, source_target_pairs={{0,1},{1,0},{2,3},{3,2},{4,5},{5,4},{6,7},{7,6},{8,9},{9,8},{10,11... | collective-permute-start | bytes 1572872 | tf_op jit(solution)/shard_map/ppermute | solution.py:281
  13.8 1.5 %late_second.1 = (bf16[256,1024]{1,0:T(8,128)(2,1)S(1)}, bf16[256,1024]{1,0:T(8,128)(2,1)S(1)}) custom-call(bf16[256,1024]{1,0:T(8,128)(2,1)S(1)} %get-tuple-element.33.dq_ref, bf16[256,256]{1,0:T(8,128)(2,1)S(1)} %get-tuple-element.34.own_ref, bf16[4,1024,1024]{2,1,0:T(8,128)(2,1)S(1)} %get-tuple-element.35.wq, bf16[4,1024,256]{2,1,0:T(8,128)(2,1)S(1)} %get-tuple-element.36.wkv), custom_call_target="tpu_custom_call" | custom-call | flops 2000000000 | bytes 1000000 | tf_op jit(solution)/shard_map/late_second/pallas_call | solution.py:256
  15.4 0.1 collective-permute-start
  15.5 0.0 collective-permute-done.1.b_ref
  15.5 0.1 add_mine.1
  15.6 0.1 collective-permute-start.2
  15.7 9.7 %collective-permute-start.4 = (bf16[128,1024]{1,0:T(8,128)(2,1)S(1)}, bf16[128,1024]{1,0:T(8,128)(2,1)S(1)}, u32[]{:S(2)}, u32[]{:S(2)}) collective-permute-start(bf16[128,1024]{1,0:T(8,128)(2,1)S(1)} %get-tuple-element.49), channel_id=1, source_target_pairs={{0,252},{1,253},{2,254},{3,255},{4,0},{5,1},{6,2},{7,3},{8,4},{9,5... | collective-permute-start | bytes 786440 | tf_op jit(solution)/shard_map/ppermute | solution.py:291
  25.4 0.0 collective-permute-done.b_ref
  25.4 0.1 add_crossed.1
  25.5 0.7 %collective-permute-start.5 = (bf16[128,1024]{1,0:T(8,128)(2,1)S(1)}, bf16[128,1024]{1,0:T(8,128)(2,1)S(1)}, u32[]{:S(2)}, u32[]{:S(2)}) collective-permute-start(bf16[128,1024]{1,0:T(8,128)(2,1)S(1)} %get-tuple-element.50), channel_id=1, source_target_pairs={{0,254},{1,255},{2,252},{3,253},{4,2},{5,3},{6,0},{7,1},{8,6},{9,7... | collective-permute-start | bytes 786440 | tf_op jit(solution)/shard_map/ppermute | solution.py:291
  26.2 3.1 %early_probabilities.1 = (bf16[512,1024]{1,0:T(8,128)(2,1)S(1)}, bf16[384,1024]{1,0:T(8,128)(2,1)S(1)}, bf16[1024,128]{1,0:T(8,128)(2,1)S(1)}, bf16[1024,128]{1,...) custom-call(s32[1]{0:T(128)S(6)} %copy.10.block_ref, bf16[1,2,256,1024]{3,2,1,0:T(8,128)(2,1)} %q_hbm.3, ...), custom_call_target="tpu_custom_call" | custom-call | flops 2000000000 | bytes 1000000 | tf_op jit(solution)/shard_map/early_probabilities/pallas_call | solution.py:256
  29.4 0.0 collective-permute-done.2.refs_1_
  29.4 0.1 add_summed.1
  29.5 2.7 %collective-permute-start.3 = (bf16[128,1024]{1,0:T(8,128)(2,1)S(1)}, bf16[128,1024]{1,0:T(8,128)(2,1)S(1)}, u32[]{:S(2)}, u32[]{:S(2)}) collective-permute-start(bf16[128,1024]{1,0:T(8,128)(2,1)S(1)} %add_summed.1), channel_id=1, source_target_pairs={{0,254},{1,255},{2,252},{3,253},{4,2},{5,3},{6,0},{7,1},{8,6},{9,7... | collective-permute-start | bytes 786440 | tf_op jit(solution)/shard_map/ppermute | solution.py:291
  32.2 0.0 collective-permute-done.4.do_in
  32.2 3.7 %collective-permute-done.5.do_more = bf16[128,1024]{1,0:T(8,128)(2,1)S(1)} collective-permute-done((bf16[128,1024]{1,0:T(8,128)(2,1)S(1)}, bf16[128,1024]{1,0:T(8,128)(2,1)S(1)}, u32[]{:S(2)}, u32[]{:S(2)}) %collective-permute-start.5) | collective-permute-done | bytes 262176 | tf_op jit(solution)/shard_map/ppermute | solution.py:291
  35.9 4.8 %early_bottom.1 = (bf16[128,1024]{1,0:T(8,128)(2,1)S(1)}, bf16[128,1024]{1,0:T(8,128)(2,1)S(1)}, bf16[128,1024]{1,0:T(8,128)(2,1)S(1)}, bf16[128,1024]{1,0:T(8,128)(2,1)S(1)}, f32[768,256]{1,0:T(8,128)S(1)}) custom-call(s32[1]{0:T(128)S(6)} %copy.10.block_ref, bf16[128,1024]{1,0:T(8,128)(2,1)S(1)} %collective-permute-done.4.do_in, ...), custom_call_target="tpu_custom_call" | custom-call | flops 2000000000 | bytes 1000000 | tf_op jit(solution)/shard_map/early_bottom/pallas_call | solution.py:256
  40.7 3.0 %collective-permute-start.10 = (bf16[128,1024]{1,0:T(8,128)(2,1)S(1)}, bf16[128,1024]{1,0:T(8,128)(2,1)S(1)}, u32[]{:S(2)}, u32[]{:S(2)}) collective-permute-start(bf16[128,1024]{1,0:T(8,128)(2,1)S(1)} %get-tuple-element.62), channel_id=1, source_target_pairs={{0,1},{1,0},{2,3},{3,2},{4,5},{5,4},{6,7},{7,6},{8,9},{9,8},{10,11... | collective-permute-start | bytes 786440 | tf_op jit(solution)/shard_map/ppermute | solution.py:281
  43.7 0.0 collective-permute-done.3.do_in
  43.7 4.6 %early_top.1 = (bf16[128,1024]{1,0:T(8,128)(2,1)S(1)}, bf16[128,1024]{1,0:T(8,128)(2,1)S(1)}, bf16[128,1024]{1,0:T(8,128)(2,1)S(1)}, bf16[128,1024]{1,0:T(8,128)(2,1)S(1)}, bf16[1,768,256]{2,1,0:T(8,128)(2,1)}) custom-call(s32[1]{0:T(128)S(6)} %copy.10.block_ref, bf16[128,1024]{1,0:T(8,128)(2,1)S(1)} %collective-permute-done.3.do_in, ...), custom_call_target="tpu_custom_call" | custom-call | flops 2000000000 | bytes 1000000 | tf_op jit(solution)/shard_map/early_top/pallas_call | solution.py:256
  48.3 0.0 collective-permute-start.8
  48.3 0.5 collective-permute-start.7
  48.8 0.0 collective-permute-start.6
  48.8 0.0 collective-permute-done.10
  48.8 0.1 add_convert_fusion
  48.9 1.1 %collective-permute-start.11 = (bf16[128,1024]{1,0:T(8,128)(2,1)S(1)}, bf16[128,1024]{1,0:T(8,128)(2,1)S(1)}, u32[]{:S(2)}, u32[]{:S(2)}) collective-permute-start(bf16[128,1024]{1,0:T(8,128)(2,1)S(1)} %add_convert_fusion), channel_id=1, source_target_pairs={{0,2},{1,3},{2,0},{3,1},{4,6},{5,7},{6,4},{7,5},{8,10},{9,11},{10,... | collective-permute-start | bytes 786440 | tf_op jit(solution)/shard_map/ppermute | solution.py:281
  50.0 0.0 collective-permute-done.8
  50.0 0.1 add_convert_fusion.1
  50.1 0.9 %collective-permute-start.9 = (bf16[128,1024]{1,0:T(8,128)(2,1)S(1)}, bf16[128,1024]{1,0:T(8,128)(2,1)S(1)}, u32[]{:S(2)}, u32[]{:S(2)}) collective-permute-start(bf16[128,1024]{1,0:T(8,128)(2,1)S(1)} %add_convert_fusion.1), channel_id=1, source_target_pairs={{0,2},{1,3},{2,0},{3,1},{4,6},{5,7},{6,4},{7,5},{8,10},{9,11},{10,... | collective-permute-start | bytes 786440 | tf_op jit(solution)/shard_map/ppermute | solution.py:281
  51.0 0.0 collective-permute-done.7.got_b
  51.0 0.0 collective-permute-done.6.got_t
  51.0 5.3 %collective-permute-done.11.refs_1_ = bf16[128,1024]{1,0:T(8,128)(2,1)S(1)} collective-permute-done((bf16[128,1024]{1,0:T(8,128)(2,1)S(1)}, bf16[128,1024]{1,0:T(8,128)(2,1)S(1)}, u32[]{:S(2)}, u32[]{:S(2)}) %collective-permute-start.11) | collective-permute-done | bytes 262176 | tf_op jit(solution)/shard_map/ppermute | solution.py:281
  56.3 5.6 %collective-permute-done.9.refs_0_ = bf16[128,1024]{1,0:T(8,128)(2,1)S(1)} collective-permute-done((bf16[128,1024]{1,0:T(8,128)(2,1)S(1)}, bf16[128,1024]{1,0:T(8,128)(2,1)S(1)}, u32[]{:S(2)}, u32[]{:S(2)}) %collective-permute-start.9) | collective-permute-done | bytes 262176 | tf_op jit(solution)/shard_map/ppermute | solution.py:281
  62.0 1.0 %finish.1 = bf16[1,256,1024]{2,1,0:T(8,128)(2,1)} custom-call(bf16[128,1024]{1,0:T(8,128)(2,1)S(1)} %get-tuple-element.55.keep_t, bf16[128,1024]{1,0:T(8,128)(2,1)S(1)} %collective-permute-done.6.got_t, bf16[128,1024]{1,0:T(8,128)(2,1)S(1)} %get-tuple-element.57.keep_b, bf16[128,1024]{1,0:T(8,128)(2,1)S(1)} %collective-permute-done.7.got_b, ...), custom_call_target="tpu_custom_call" | custom-call | flops 2000000000 | bytes 1000000 | tf_op jit(solution)/shard_map/finish/pallas_call | solution.py:256
Async XLA Ops:
  10.5 5.0 %collective-permute-start.1 = (bf16[256,1024]{1,0:T(8,128)(2,1)S(1)}, bf16[256,1024]{1,0:T(8,128)(2,1)S(1)}, u32[]{:S(2)}, u32[]{:S(2)}) collective-permute-start(bf16[256,1024]{1,0:T(8,128)(2,1)S(1)} %get-tuple-element.43), channel_id=1, source_target_pairs={{0,1},{1,0},{2,3},{3,2},{4,5},{5,4},{6,7},{7,6},{8,9},{9,8},{10,11... | collective-permute-start | bytes 1572872 | tf_op jit(solution)/shard_map/ppermute | solution.py:281
  15.4 10.0 %collective-permute-start = (bf16[256,1024]{1,0:T(8,128)(2,1)S(1)}, bf16[256,1024]{1,0:T(8,128)(2,1)S(1)}, u32[]{:S(2)}, u32[]{:S(2)}) collective-permute-start(bf16[256,1024]{1,0:T(8,128)(2,1)S(1)} %get-tuple-element.38), channel_id=1, source_target_pairs={{0,1},{1,0},{2,3},{3,2},{4,5},{5,4},{6,7},{7,6},{8,9},{9,8},{10,11... | collective-permute-start | bytes 1572872 | tf_op jit(solution)/shard_map/ppermute | solution.py:281
  15.6 13.8 %collective-permute-start.2 = (bf16[128,1024]{1,0:T(8,128)(2,1)S(1)}, bf16[128,1024]{1,0:T(8,128)(2,1)S(1)}, u32[]{:S(2)}, u32[]{:S(2)}) collective-permute-start(bf16[128,1024]{1,0:T(8,128)(2,1)S(1)} %get-tuple-element.44), channel_id=1, source_target_pairs={{0,2},{1,3},{2,0},{3,1},{4,6},{5,7},{6,4},{7,5},{8,10},{9,11},{10,... | collective-permute-start | bytes 786440 | tf_op jit(solution)/shard_map/ppermute | solution.py:281
  15.7 16.5 %collective-permute-start.4 = (bf16[128,1024]{1,0:T(8,128)(2,1)S(1)}, bf16[128,1024]{1,0:T(8,128)(2,1)S(1)}, u32[]{:S(2)}, u32[]{:S(2)}) collective-permute-start(bf16[128,1024]{1,0:T(8,128)(2,1)S(1)} %get-tuple-element.49), channel_id=1, source_target_pairs={{0,252},{1,253},{2,254},{3,255},{4,0},{5,1},{6,2},{7,3},{8,4},{9,5... | collective-permute-start | bytes 786440 | tf_op jit(solution)/shard_map/ppermute | solution.py:291
  25.5 10.4 %collective-permute-start.5 = (bf16[128,1024]{1,0:T(8,128)(2,1)S(1)}, bf16[128,1024]{1,0:T(8,128)(2,1)S(1)}, u32[]{:S(2)}, u32[]{:S(2)}) collective-permute-start(bf16[128,1024]{1,0:T(8,128)(2,1)S(1)} %get-tuple-element.50), channel_id=1, source_target_pairs={{0,254},{1,255},{2,252},{3,253},{4,2},{5,3},{6,0},{7,1},{8,6},{9,7... | collective-permute-start | bytes 786440 | tf_op jit(solution)/shard_map/ppermute | solution.py:291
  29.5 14.2 %collective-permute-start.3 = (bf16[128,1024]{1,0:T(8,128)(2,1)S(1)}, bf16[128,1024]{1,0:T(8,128)(2,1)S(1)}, u32[]{:S(2)}, u32[]{:S(2)}) collective-permute-start(bf16[128,1024]{1,0:T(8,128)(2,1)S(1)} %add_summed.1), channel_id=1, source_target_pairs={{0,254},{1,255},{2,252},{3,253},{4,2},{5,3},{6,0},{7,1},{8,6},{9,7... | collective-permute-start | bytes 786440 | tf_op jit(solution)/shard_map/ppermute | solution.py:291
  40.7 8.1 %collective-permute-start.10 = (bf16[128,1024]{1,0:T(8,128)(2,1)S(1)}, bf16[128,1024]{1,0:T(8,128)(2,1)S(1)}, u32[]{:S(2)}, u32[]{:S(2)}) collective-permute-start(bf16[128,1024]{1,0:T(8,128)(2,1)S(1)} %get-tuple-element.62), channel_id=1, source_target_pairs={{0,1},{1,0},{2,3},{3,2},{4,5},{5,4},{6,7},{7,6},{8,9},{9,8},{10,11... | collective-permute-start | bytes 786440 | tf_op jit(solution)/shard_map/ppermute | solution.py:281
  48.3 1.8 %collective-permute-start.8 = (bf16[128,1024]{1,0:T(8,128)(2,1)S(1)}, bf16[128,1024]{1,0:T(8,128)(2,1)S(1)}, u32[]{:S(2)}, u32[]{:S(2)}) collective-permute-start(bf16[128,1024]{1,0:T(8,128)(2,1)S(1)} %get-tuple-element.60), channel_id=1, source_target_pairs={{0,1},{1,0},{2,3},{3,2},{4,5},{5,4},{6,7},{7,6},{8,9},{9,8},{10,11... | collective-permute-start | bytes 786440 | tf_op jit(solution)/shard_map/ppermute | solution.py:281
  48.3 2.7 %collective-permute-start.7 = (bf16[128,1024]{1,0:T(8,128)(2,1)S(1)}, bf16[128,1024]{1,0:T(8,128)(2,1)S(1)}, u32[]{:S(2)}, u32[]{:S(2)}) collective-permute-start(bf16[128,1024]{1,0:T(8,128)(2,1)S(1)} %get-tuple-element.58), channel_id=1, source_target_pairs={{0,1},{1,0},{2,3},{3,2},{4,5},{5,4},{6,7},{7,6},{8,9},{9,8},{10,11... | collective-permute-start | bytes 786440 | tf_op jit(solution)/shard_map/ppermute | solution.py:281
  48.8 2.2 %collective-permute-start.6 = (bf16[128,1024]{1,0:T(8,128)(2,1)S(1)}, bf16[128,1024]{1,0:T(8,128)(2,1)S(1)}, u32[]{:S(2)}, u32[]{:S(2)}) collective-permute-start(bf16[128,1024]{1,0:T(8,128)(2,1)S(1)} %get-tuple-element.56), channel_id=1, source_target_pairs={{0,1},{1,0},{2,3},{3,2},{4,5},{5,4},{6,7},{7,6},{8,9},{9,8},{10,11... | collective-permute-start | bytes 786440 | tf_op jit(solution)/shard_map/ppermute | solution.py:281
  48.9 7.5 %collective-permute-start.11 = (bf16[128,1024]{1,0:T(8,128)(2,1)S(1)}, bf16[128,1024]{1,0:T(8,128)(2,1)S(1)}, u32[]{:S(2)}, u32[]{:S(2)}) collective-permute-start(bf16[128,1024]{1,0:T(8,128)(2,1)S(1)} %add_convert_fusion), channel_id=1, source_target_pairs={{0,2},{1,3},{2,0},{3,1},{4,6},{5,7},{6,4},{7,5},{8,10},{9,11},{10,... | collective-permute-start | bytes 786440 | tf_op jit(solution)/shard_map/ppermute | solution.py:281
  50.1 11.9 %collective-permute-start.9 = (bf16[128,1024]{1,0:T(8,128)(2,1)S(1)}, bf16[128,1024]{1,0:T(8,128)(2,1)S(1)}, u32[]{:S(2)}, u32[]{:S(2)}) collective-permute-start(bf16[128,1024]{1,0:T(8,128)(2,1)S(1)} %add_convert_fusion.1), channel_id=1, source_target_pairs={{0,2},{1,3},{2,0},{3,1},{4,6},{5,7},{6,4},{7,5},{8,10},{9,11},{10,... | collective-permute-start | bytes 786440 | tf_op jit(solution)/shard_map/ppermute | solution.py:281
